TPU v7x, 256 devices: a whole 4x4x8 slice. The times are simulated.
256 devices in a mesh: tp: 16 (over z_lo, x), dp: 16 (over y, z_hi, core).
Axes of the slice: x: 4, y: 4, z: 8 (z_hi: 2, z_lo: 4; z = z_hi * 4 + z_lo), core: 2. Of those that a mesh axis runs over, the one named last changes fastest.
Arguments:
- img_tokens: bfloat16 [256, 64, 5120], P(None, 'dp', 'tp'), may hold values from -6 to 6
- key_weight: bfloat16 [5120, 5120], P('tp'), may hold values from -0.078125 to 0.078125
- value_map: bfloat16 [5120, 40], P('tp'), may hold values from -0.15625 to 0.15625
- queries: bfloat16 [256, 32, 5120], P('dp'), may hold values from -216 to 216
- cap_lengths: int32 [256], P('dp'), may hold values from 1 to 32
- candidates: int32 [64, 8], P('dp'), may hold values from 0 to 255, as said below
- counts: int32 [64], P('dp'), may hold values from 1 to 8
Outputs:
- pair_scores: float32 [64, 8], P('dp')
Inputs may be any that keep to these rules, and one draw needn't show every extreme that they name: `candidates`: for every index g of dp and every index o of dp, exactly 2 of the 4 x 8 candidate slots (used or not) held at index g name a caption among o * 16 to (o + 1) * 16 - 1; the same caption may appear in several slots.
All inputs are finite; a program needn't handle non-finite values.
Results may differ from a plain program's by a relative error of at most 0.0003.
Values may be sent and summed in bfloat16 or wider, within the bound.
No kernel may reach another device: no remote copies, remote signals or barrier semaphores. Data moves between devices by JAX's collectives and lax.ppermute only.
A program may use at most 192 MiB of HBM per device.

v0:
```python
import jax
import jax.numpy as jnp
from jax import lax
from jax.sharding import PartitionSpec as P

H = 40
HD = 128
L = 32
TOP = 8
CAP_DP = 16


def merged(shard, axis, combine):
    everything = jax.tree.map(lambda part: lax.all_gather(part, axis), shard)
    initial = jax.tree.map(lambda part: part[0], everything)

    def turn(k, so_far):
        return combine(so_far, jax.tree.map(lambda part: part[k], everything))

    return lax.fori_loop(1, lax.axis_size(axis), turn, initial)


def softmax_join(first_part, second_part):
    peak = jnp.maximum(first_part[0], second_part[0])
    first_factor = jnp.exp(first_part[0] - peak)
    second_factor = jnp.exp(second_part[0] - peak)
    totals = first_part[1] * first_factor + second_part[1] * second_factor
    weighted = first_part[2] * first_factor + second_part[2] * second_factor
    return (peak, totals, weighted)


def local(img_tokens, key_weight, value_map, queries, cap_lengths, candidates, counts):
    patch_count, img_here, col_width = img_tokens.shape
    tp_count = lax.axis_size("tp")
    dp_count = lax.axis_size("dp")
    token_rows = img_tokens.reshape(patch_count * img_here, col_width)
    patches_here = patch_count // tp_count
    row_block = token_rows
    key_block = lax.psum_scatter(
        jnp.dot(row_block, key_weight, preferred_element_type=jnp.float32),
        "tp",
        scatter_dimension=0,
        tiled=True,
    )
    row_block = token_rows
    value_block = lax.psum_scatter(
        jnp.dot(row_block, value_map, preferred_element_type=jnp.float32),
        "tp",
        scatter_dimension=0,
        tiled=True,
    )
    slot_total = img_here * TOP
    per_owner = slot_total // dp_count
    cand_ids = candidates.reshape(slot_total)
    owners = cand_ids // CAP_DP
    local_ids = cand_ids % CAP_DP
    slot_order = jnp.arange(slot_total, dtype=jnp.int32)
    same_owner = owners[:, None] == owners[None, :]
    earlier = slot_order[:, None] > slot_order[None, :]
    slot_rank = jnp.sum((same_owner & earlier).astype(jnp.int32), axis=1)
    owner_hot = owners[:, None] == jnp.arange(dp_count, dtype=jnp.int32)[None, :]
    rank_hot = slot_rank[:, None] == jnp.arange(per_owner, dtype=jnp.int32)[None, :]
    requests = jnp.sum(
        jnp.where(owner_hot[:, :, None] & rank_hot[:, None, :], local_ids[:, None, None], 0), axis=0
    )
    asked_ids = lax.all_to_all(requests, "dp", split_axis=0, concat_axis=0, tiled=True)
    picked_rows = queries[asked_ids]
    picked_lengths = cap_lengths[asked_ids]
    replies = lax.all_to_all(picked_rows, "dp", split_axis=0, concat_axis=0, tiled=True)
    length_back = lax.all_to_all(picked_lengths, "dp", split_axis=0, concat_axis=0, tiled=True)
    reply_width = replies.shape[3]
    flat_index = owners * per_owner + slot_rank
    slot_queries = replies.reshape(dp_count * per_owner, L, reply_width)[flat_index]
    slot_lengths = length_back.reshape(dp_count * per_owner)[flat_index]
    attn_scale = float(HD) ** (-0.5)
    query_block = slot_queries.reshape(img_here, TOP, L, H, HD).astype(jnp.float32)
    image_keys = key_block.reshape(patches_here, img_here, H, HD)
    values_here = jnp.swapaxes(value_block.reshape(patches_here, img_here, H), 0, 1)
    logits = (
        jnp.einsum("jklhd,pjhd->jkhlp", query_block, image_keys, precision=lax.Precision.HIGHEST)
        * attn_scale
    )
    local_peak = jnp.max(logits, axis=-1)
    weights = jnp.exp(logits - local_peak[..., None])
    local_totals = jnp.sum(weights, axis=-1)
    local_weighted = jnp.einsum(
        "jkhlp,jph->jkhl", weights, values_here, precision=lax.Precision.HIGHEST
    )
    peak, totals, weighted = merged((local_peak, local_totals, local_weighted), "tp", softmax_join)
    attended = weighted / totals
    lengths_here = slot_lengths.reshape(img_here, TOP)
    token_live = (jnp.arange(L, dtype=jnp.int32)[None, None, :] < lengths_here[:, :, None]).astype(
        jnp.float32
    )
    pair_score = jnp.sum(attended * token_live[:, :, None, :], axis=(2, 3)) / lengths_here.astype(
        jnp.float32
    )
    slot_live = jnp.arange(TOP, dtype=jnp.int32)[None, :] < counts[:, None]
    return jnp.where(slot_live, pair_score, jnp.zeros_like(pair_score))


def solution(mesh):
    in_specs = (
        P(None, "dp", "tp"),
        P("tp", None),
        P("tp", None),
        P("dp", None, None),
        P("dp"),
        P("dp", None),
        P("dp"),
    )
    out_specs = P("dp", None)
    return jax.shard_map(local, mesh=mesh, in_specs=in_specs, out_specs=out_specs, check_vma=False)
```

profile of v0, /device:TPU:8, one launch (start us, length us, event | category | flops | bytes accessed | tf_op | source)
XLA Modules:
  0.0 991.6 jit_solution(7065666456682143612)
XLA Ops:
  6.5 2.3 copy.33
  8.8 2.3 reshape.248
  11.1 11.0 %fusion.12 = f32[1024,5120]{1,0:T(8,128)} fusion(bf16[1024,320]{1,0:T(8,128)(2,1)} %reshape.248, bf16[320,5120]{1,0:T(8,128)(2,1)S(1)} %copy-done), kind=kOutput, calls=%fused_computation.50 | convolution fusion | flops 3355443200 | bytes 24903680 | tf_op jit(solution)/shard_map/dot_general | solution.py:40
  23.3 19.9 %all_to_all.26 = s32[16,1,2]{2,1,0:T(1,128)S(1)} all-to-all(s32[16,1,2]{2,1,0:T(1,128)S(1)} %copy.34), channel_id=1, replica_groups=mesh['tp'=16,'dp'=16] {'dp'}, dimensions={0} | all-to-all | bytes 256 | tf_op jit(solution)/shard_map/all_to_all | solution.py:66
  43.5 8.4 gather_fusion
  52.0 6.2 all-to-all-start.1
  59.6 231.7 %all-to-all-done.1 = bf16[16,2,32,5120]{3,2,1,0:T(8,128)(2,1)} async-done(((bf16[16,2,32,5120]{3,2,1,0:T(8,128)(2,1)}), bf16[16,2,32,5120]{3,2,1,0:T(8,128)(2,1)}, u32[]{:S(2)}, u32[]{:S(2)}) %all-to-all-start.1) | async-done | bytes 10485792 | tf_op jit(solution)/shard_map/all_to_all | solution.py:69
  291.2 9.9 %gather_fusion.1 = bf16[32,32,5120]{2,1,0:T(8,128)(2,1)} fusion(bf16[32,32,5120]{2,1,0:T(8,128)(2,1)} %bitcast.9, s32[1024]{0:T(1024)S(1)} %pad_clamp_fusion), kind=kCustom, calls=%fused_computation.1 | custom fusion | bytes 20971648 | tf_op jit(solution)/shard_map/gather | solution.py:73
  301.2 11.2 %copy.67 = bf16[128,8,40,128]{3,2,1,0:T(8,128)(2,1)} copy(bf16[128,8,40,128]{3,1,2,0:T(8,128)(2,1)} %bitcast.74) | data formatting | bytes 20971520
  312.3 169.6 %reduce-scatter.5.cloned.1.call-done = f32[64,5120]{1,0:T(8,128)} async-done(((f32[1024,5120]{1,0:T(8,128)}), f32[64,5120]{1,0:T(8,128)}) %reduce-scatter.5.cloned.1.call-update) | async-done | bytes 1310736 | tf_op jit(solution)/shard_map/reduce_scatter | solution.py:39
  481.9 1.5 copy.66
  483.4 45.9 %bitcast_reduce_fusion = (f32[4,8,40,32]{3,1,2,0:T(8,128)S(1)}, f32[4,40,16,8,32]{4,2,3,1,0:T(8,128)}) fusion(bf16[4,8,32,40,128]{4,3,2,1,0:T(8,128)(2,1)} %bitcast.72, f32[16,4,40,128,1]{3,2,1,0,4:T(8,128)S(1)} %bitcast.75), kind=kOutput, calls=%fused_computation.16 | convolution fusion | flops 1007902720 | bytes 14581760 | tf_op jit(solution)/shard_map/jklhd,pjhd->jkhlp/dot_general | solution.py:80
  530.5 7.9 fusion.6
  539.5 24.8 %reduce-scatter.7.cloned.1.call-done = f32[64,40]{1,0:T(8,128)} async-done(((f32[1024,40]{1,0:T(8,128)}), f32[64,40]{1,0:T(8,128)}) %reduce-scatter.7.cloned.1.call-update) | async-done | bytes 10256 | tf_op jit(solution)/shard_map/reduce_scatter | solution.py:46
  565.2 6.6 multiply_reduce_fusion
  574.3 7.4 all-to-all-start.2
  581.7 8.6 all-to-all-done.2
  592.5 72.6 %all-gather.7.cloned.1.call-done = f32[64,8,40,32]{2,3,1,0:T(8,128)} async-done(((f32[4,8,40,32]{2,3,1,0:T(8,128)}), f32[64,8,40,32]{2,3,1,0:T(8,128)}) %all-gather.7.cloned.1.call-update) | async-done | bytes 2621456 | tf_op jit(solution)/shard_map/all_gather | solution.py:14
  666.4 99.6 %all-gather.9.cloned.1.call-done = f32[64,8,40,32]{2,3,1,0:T(8,128)} async-done(((f32[4,8,40,32]{2,3,1,0:T(8,128)}), f32[64,8,40,32]{2,3,1,0:T(8,128)}) %all-gather.9.cloned.1.call-update) | async-done | bytes 2621456 | tf_op jit(solution)/shard_map/all_gather | solution.py:14
  768.3 98.8 %all-gather.11.cloned.1.call-done = f32[64,8,40,32]{2,3,1,0:T(8,128)} async-done(((f32[4,8,40,32]{2,3,1,0:T(8,128)}), f32[64,8,40,32]{2,3,1,0:T(8,128)}) %all-gather.11.cloned.1.call-update) | async-done | bytes 2621456 | tf_op jit(solution)/shard_map/all_gather | solution.py:14
  869.3 113.5 %while.19 = (s32[]{:T(128)}, f32[4,8,40,32]{3,2,1,0:T(8,128)S(1)}, f32[4,8,40,32]{3,2,1,0:T(8,128)}, f32[4,8,40,32]{3,2,1,0:T(8,128)}, f32[16,4,8,40,32]{3,4,2,1...) while((s32[]{:T(128)}, f32[4,8,40,32]{3,2,1,0:T(8,128)S(1)}, ...), condition=%wide.region_7.8_spmd, body=%wide.region_6.7_spmd.sunk | while | flops 450565 | bytes 4259983 | solution.py:20
  870.6 1.3 constant_dynamic-slice_fusion.5
  872.4 2.2 fusion.20
  874.6 2.2 fusion.21
  878.2 1.3 constant_dynamic-slice_fusion.5
  880.0 2.2 fusion.20
  882.2 2.2 fusion.21
  885.7 1.3 constant_dynamic-slice_fusion.5
  887.5 2.2 fusion.20
  889.7 2.2 fusion.21
  893.3 1.3 constant_dynamic-slice_fusion.5
  895.1 2.2 fusion.20
  897.3 2.2 fusion.21
  900.9 1.3 constant_dynamic-slice_fusion.5
  902.7 2.2 fusion.20
  904.9 2.2 fusion.21
  908.4 1.3 constant_dynamic-slice_fusion.5
  910.2 2.2 fusion.20
  912.4 2.2 fusion.21
  916.0 1.3 constant_dynamic-slice_fusion.5
  917.8 2.2 fusion.20
  920.0 2.2 fusion.21
  923.6 1.3 constant_dynamic-slice_fusion.5
  925.4 2.2 fusion.20
  927.5 2.2 fusion.21
  931.1 1.3 constant_dynamic-slice_fusion.5
  932.9 2.2 fusion.20
  935.1 2.2 fusion.21
  940.5 2.2 fusion.20
  942.7 2.2 fusion.21
  948.1 2.2 fusion.20
  950.2 2.2 fusion.21
  953.8 1.3 constant_dynamic-slice_fusion.5
  955.6 2.2 fusion.20
  957.8 2.2 fusion.21
  961.4 1.3 constant_dynamic-slice_fusion.5
  963.2 2.2 fusion.20
  965.4 2.2 fusion.21
  969.0 1.3 constant_dynamic-slice_fusion.5
  970.8 2.2 fusion.20
  972.9 2.2 fusion.21
  978.3 2.2 fusion.20
  980.5 2.2 fusion.21
  982.7 1.7 multiply_reduce_fusion.1
  (137 shorter events, 49.2 us)
Async XLA Ops:
  6.5 4.6 copy-start
  6.5 475.4 %reduce-scatter.5.cloned.1.call-start = ((), (), s32[]{:S(2)}) async-start(), calls=%async_computation.5 | async-start | bytes 22282240 | tf_op jit(solution)/shard_map/reduce_scatter | solution.py:39
  22.1 0.7 copy-start.5
  52.0 6.2 copy-start.3
  52.0 6.2 copy-start.4
  52.0 239.2 %all-to-all-start.1 = ((bf16[16,2,32,5120]{3,2,1,0:T(8,128)(2,1)}), bf16[16,2,32,5120]{3,2,1,0:T(8,128)(2,1)}, u32[]{:S(2)}, u32[]{:S(2)}) async-start(bf16[16,2,32,5120]{3,2,1,0:T(8,128)(2,1)} %bitcast.73), calls=%async_computation.2 | async-start | bytes 20971520 | tf_op jit(solution)/shard_map/all_to_all | solution.py:69
  58.2 506.2 %reduce-scatter.7.cloned.1.call-start = ((), (), s32[]{:S(2)}) async-start(), calls=%async_computation.9 | async-start | bytes 557056 | tf_op jit(solution)/shard_map/reduce_scatter | solution.py:46
  59.4 605.7 %all-gather.7.cloned.1.call-start = ((), (), s32[]{:S(2)}) async-start(), calls=%async_computation.6 | async-start | bytes 8912896 | tf_op jit(solution)/shard_map/all_gather | solution.py:14
  530.5 235.6 %all-gather.9.cloned.1.call-start = ((), (), s32[]{:S(2)}) async-start(), calls=%async_computation.7 | async-start | bytes 8912896 | tf_op jit(solution)/shard_map/all_gather | solution.py:14
  538.4 34.5 %copy-start.2 = (s32[16]{0:T(128)S(1)}, s32[16]{0:T(128)}, u32[]{:S(2)}) copy-start(s32[16]{0:T(128)} %param.13) | copy-start | bytes 196
  539.5 327.5 %all-gather.11.cloned.1.call-start = ((), (), s32[]{:S(2)}) async-start(), calls=%async_computation.8 | async-start | bytes 8912896 | tf_op jit(solution)/shard_map/all_gather | solution.py:14
  574.3 15.9 %all-to-all-start.2 = ((s32[16,1,2]{2,1,0:T(1,128)}), s32[16,1,2]{2,1,0:T(1,128)S(1)}, u32[]{:S(2)}, u32[]{:S(2)}) async-start(s32[16,1,2]{2,1,0:T(1,128)} %bitcast.21), calls=%async_computation.3 | async-start | bytes 16384 | tf_op jit(solution)/shard_map/all_to_all | solution.py:70
  869.3 115.2 %copy-start.6 = (s32[4]{0:T(128)S(1)}, s32[4]{0:T(128)}, u32[]{:S(2)}) copy-start(s32[4]{0:T(128)} %param.15) | copy-start | bytes 52
  982.7 2.4 copy-start.1
Sparse Core Ops, SparseCore 0:
  22.3 459.5 reduce-scatter.4
  484.4 79.9 reduce-scatter.6
  566.3 98.7 all-gather.6
  666.9 99.1 all-gather.8
  767.8 99.1 all-gather.10
where the time goes:
time: 996 us; the launch traced here: 992 us
  waiting for transfers between devices  706 us (71%)
  local copies, waits for them, and re-layouts  97 us (10%)
  other arithmetic  83.2 us (8%)
  matrix products  58.1 us (6%)
  blocking collectives  19.9 us (2%)
  starting transfers between devices  13.7 us (1%)
  between operations  13.3 us (1%)
    all_gather x3, waiting for transfers between devices, merged(): everything = jax.tree.map(lambda part: lax.all_gather(part, axis), shard)  271 us
    all_to_all x1, waiting for transfers between devices, local(): lax.all_to_all(picked_rows, 'dp', split_axis=0, concat_axis=0, tiled=True)  232 us
    reduce_scatter x1, waiting for transfers between devices, local(): lax.psum_scatter(jnp.dot(row_block, key_weight, preferred_element_type=jn...  170 us
    dynamic_slice x75, local copies, waits for them, and re-layouts, turn(): return combine(so_far, jax.tree.map(lambda part: part[k], everything))  46.9 us
    dot_general x1, matrix products, local(): jnp.einsum('jklhd,pjhd->jkhlp', query_block, image_keys, precision=lax.Pr...  45.9 us
    add x15, other arithmetic, softmax_join(): weighted = first_part[2] * first_factor + second_part[2] * second_factor  32.7 us
    add x15, other arithmetic, softmax_join(): totals = first_part[1] * first_factor + second_part[1] * second_factor  32.5 us
    reduce_scatter x1, waiting for transfers between devices, local(): lax.psum_scatter(jnp.dot(row_block, value_map, preferred_element_type=jnp...  24.8 us
  transfers between devices with their start and end apart: 7, of which 7 were waited for; matrix products, arithmetic and copies ran while one was open for 10% of the time, Pallas kernels for 0%

commit v1 on v0

v1 whole, which is shorter than its diff:
```python
import functools

import jax
import jax.numpy as jnp
from jax import lax
from jax.experimental import pallas as pl
from jax.experimental.pallas import tpu as pltpu
from jax.sharding import Mesh
from jax.sharding import PartitionSpec as P

H = 40
HD = 128
L = 32
TOP = 8
CAP_DP = 16
IMG = 4
GROUPS = 8
GH = H // GROUPS
GW = GH * HD
PATCH = 256
FEAT = 320
WIDE = 2 * FEAT
TP = ("zl", "x")
DP = ("y", "zh", "c")
YC = ("y", "c")


def pick_kernel(ids, col, q_ref, o_ref, sem):
    start = pl.multiple_of(col[0] * GW, 128)
    copies = []
    for r in range(2 * CAP_DP):
        copies.append(
            pltpu.make_async_copy(q_ref.at[ids[r], :, pl.ds(start, GW)], o_ref.at[r], sem.at[r])
        )
    for c in copies:
        c.start()
    for c in copies:
        c.wait()


def pick_queries(queries, ids, col):
    return pl.pallas_call(
        pick_kernel,
        out_shape=jax.ShapeDtypeStruct((2 * CAP_DP, L, GW), queries.dtype),
        in_specs=[
            pl.BlockSpec(memory_space=pltpu.SMEM),
            pl.BlockSpec(memory_space=pltpu.SMEM),
            pl.BlockSpec(memory_space=pl.ANY),
        ],
        out_specs=pl.BlockSpec(memory_space=pl.ANY),
        scratch_shapes=[pltpu.SemaphoreType.DMA((2 * CAP_DP,))],
        cost_estimate=pl.CostEstimate(flops=0, bytes_accessed=2 * 1310720, transcendentals=0),
        name="pick_queries",
    )(ids, col, queries)


def attend_kernel(order, slot, *refs):
    units = refs[:16]
    w_ref, v_ref, q_ref, o_ref = refs[16:20]
    xs, ws, vs, qs, acc, val, xsem, wsem, osem = refs[20:]
    xcopy = [pltpu.make_async_copy(units[u], xs.at[u], xsem.at[u]) for u in range(16)]
    wcopy = [pltpu.make_async_copy(w_ref.at[:, order[u]], ws.at[u], wsem.at[u]) for u in range(16)]
    vcopy = pltpu.make_async_copy(v_ref, vs, osem.at[0])
    qcopy = pltpu.make_async_copy(q_ref, qs, osem.at[1])
    vcopy.start()
    for u in range(16):
        wcopy[u].start()
        xcopy[u].start()
    qcopy.start()
    vcopy.wait()
    lane = lax.broadcasted_iota(jnp.int32, (PATCH, HD), 1)
    low = lane < HD // 2

    def rows_of(u):
        full = xs[u]
        rest = full[:, 512:640]
        zero = jnp.zeros_like(rest)
        first = jnp.concatenate([full[:, 0:256], jnp.where(low, rest, zero)], axis=1)
        second = jnp.concatenate([full[:, 256:512], jnp.where(low, zero, rest)], axis=1)
        return jnp.concatenate([first, second], axis=0)

    def weights_of(u):
        w = ws[u].astype(jnp.float32).reshape(FEAT, GW).astype(jnp.bfloat16)
        v = vs[order[u]]
        v = jnp.concatenate([v, v[:, 256:320]], axis=1)
        return jnp.concatenate([w, w[256:320]], axis=0), v

    for pair in range(8):
        a, b = 2 * pair, 2 * pair + 1
        for u in (a, b):
            wcopy[u].wait()
            xcopy[u].wait()
        x = jnp.concatenate([rows_of(a), rows_of(b)], axis=1)
        (wa, va), (wb, vb) = weights_of(a), weights_of(b)
        w = jnp.concatenate([wa, wb], axis=0)
        v = jnp.concatenate([va, vb], axis=1)
        keys = jnp.dot(x, w, preferred_element_type=jnp.float32)
        values = lax.dot_general(
            x, v, (((1,), (1,)), ((), ())), preferred_element_type=jnp.float32
        )
        if pair == 0:
            acc[...] = keys
            val[...] = values
        else:
            acc[...] += keys
            val[...] += values
    qcopy.wait()
    scale = float(HD) ** (-0.5)
    dims = (((1,), (1,)), ((), ()))
    for i in range(2):
        q = jnp.concatenate([qs[slot[TOP * i + k]] for k in range(TOP)], axis=0)
        total = jnp.zeros((1, TOP * L), jnp.float32)
        for h in range(GH):
            k = acc[PATCH * i : PATCH * (i + 1), HD * h : HD * (h + 1)]
            qh = q[:, HD * h : HD * (h + 1)]
            k1 = k.astype(jnp.bfloat16)
            r1 = k - k1.astype(jnp.float32)
            k2 = r1.astype(jnp.bfloat16)
            k3 = (r1 - k2.astype(jnp.float32)).astype(jnp.bfloat16)
            part = functools.partial(
                lax.dot_general, dimension_numbers=dims, preferred_element_type=jnp.float32
            )
            logits = (part(k3, qh) + part(k2, qh) + part(k1, qh)) * scale
            peak = jnp.max(logits, axis=0, keepdims=True)
            e = jnp.exp(logits - peak)
            norm = jnp.sum(e, axis=0, keepdims=True)
            v = val[PATCH * i : PATCH * (i + 1), h : h + 1]
            total = total + jnp.sum(e * v, axis=0, keepdims=True) / norm
        o_ref[i : i + 1, :] = total


def attend(order, slot, units, w, v, q):
    bf = jnp.bfloat16
    return pl.pallas_call(
        attend_kernel,
        out_shape=jax.ShapeDtypeStruct((2, TOP * L), jnp.float32),
        in_specs=[pl.BlockSpec(memory_space=pltpu.SMEM)] * 2
        + [pl.BlockSpec(memory_space=pl.ANY)] * 19,
        out_specs=pl.BlockSpec(memory_space=pltpu.VMEM),
        scratch_shapes=[
            pltpu.VMEM((16, PATCH, WIDE), bf),
            pltpu.VMEM((16, GROUPS, FEAT // 8, GW), bf),
            pltpu.VMEM((16, 8, FEAT), bf),
            pltpu.VMEM((2 * CAP_DP, L, GW), bf),
            pltpu.VMEM((2 * PATCH, GW), jnp.float32),
            pltpu.VMEM((2 * PATCH, 8), jnp.float32),
            pltpu.SemaphoreType.DMA((16,)),
            pltpu.SemaphoreType.DMA((16,)),
            pltpu.SemaphoreType.DMA((2,)),
        ],
        compiler_params=pltpu.CompilerParams(vmem_limit_bytes=44 * 2**20),
        cost_estimate=pl.CostEstimate(
            flops=2 * 512 * 5120 * 640, bytes_accessed=13 * 2**20, transcendentals=655360
        ),
        name="attend",
    )(order, slot, *units, w, v, q)


def shift(block, axis, by):
    return lax.ppermute(block, axis, [(i, (i + by) % 4) for i in range(4)])


def flip(block, mask):
    return lax.ppermute(block, "zl", [(i, i ^ mask) for i in range(4)])


def ring(unit):
    right = shift(unit, "x", 1)
    left = shift(unit, "x", -1)
    half = PATCH // 2
    top = shift(right[:half], "x", 1)
    bottom = shift(left[half:], "x", -1)
    return [unit, left, jnp.concatenate([top, bottom], axis=0), right]


def local(img_tokens, key_weight, value_map, queries, cap_lengths, candidates, counts):
    zl, x = lax.axis_index("zl"), lax.axis_index("x")
    half = zl // 2
    group = (zl % 2) * 4 + x
    me = lax.axis_index(DP)
    part = lax.axis_index(YC)

    slot_total = IMG * TOP
    cand_ids = candidates.reshape(slot_total)
    notice = jnp.broadcast_to(jnp.concatenate([cand_ids, cap_lengths])[None], (16, slot_total + CAP_DP))
    notices = lax.all_to_all(notice, DP, split_axis=0, concat_axis=0, tiled=True)

    tokens = img_tokens.reshape(PATCH, 2, 2, FEAT)
    packed = jnp.concatenate(
        [
            tokens[:, :, 0, :256],
            tokens[:, :, 1, :256],
            tokens[:, :, 0, 256:],
            tokens[:, :, 1, 256:],
        ],
        axis=-1,
    )
    mine = jnp.where(half == 0, packed[:, 0], packed[:, 1])
    theirs = jnp.where(half == 0, packed[:, 1], packed[:, 0])
    columns = [mine, flip(mine, 1), flip(theirs, 2), flip(theirs, 3)]
    units = [u for column in columns for u in ring(column)]
    order = jnp.stack([(zl ^ d) * 4 + (x + e) % 4 for d in range(4) for e in range(4)]).astype(jnp.int32)

    rows = FEAT // 8
    w_part = lax.dynamic_slice_in_dim(key_weight, part * rows, rows, axis=0)
    w_part = jnp.swapaxes(w_part.reshape(rows, GROUPS, GW), 0, 1)
    w_sent = jnp.concatenate([w_part, w_part], axis=0)
    w_mine = lax.all_to_all(w_sent, TP, split_axis=0, concat_axis=0, tiled=True)
    w_all = lax.all_gather(w_mine, YC)
    v_part = jnp.pad(value_map.T.reshape(GROUPS, GH, FEAT), ((0, 0), (0, 8 - GH), (0, 0)))
    v_all = lax.all_to_all(
        jnp.concatenate([v_part, v_part], axis=0), TP, split_axis=0, concat_axis=0, tiled=True
    )

    asked = notices[:, :slot_total]
    lengths = notices[:, slot_total:].reshape(16 * CAP_DP)
    match = (asked // CAP_DP) == me
    slots = jnp.arange(slot_total, dtype=jnp.int32)
    earlier = slots[:, None] > slots[None, :]
    rank = jnp.sum((match[:, None, :] & earlier[None]).astype(jnp.int32), axis=2)
    ids = jnp.sum(
        jnp.where(match[:, None, :] & (rank[:, None, :] == jnp.arange(2)[None, :, None]), asked[:, None, :] % CAP_DP, 0),
        axis=2,
    ).reshape(2 * CAP_DP)
    picked = pick_queries(queries, ids.astype(jnp.int32), group[None].astype(jnp.int32))
    replies = lax.all_to_all(
        picked.reshape(16, 2, L, GW), DP, split_axis=0, concat_axis=0, tiled=True
    ).reshape(2 * CAP_DP, L, GW)
    owners = cand_ids // CAP_DP
    own_rank = jnp.sum(((owners[:, None] == owners[None, :]) & earlier).astype(jnp.int32), axis=1)
    flat = (owners * 2 + own_rank).astype(jnp.int32)
    slot = jnp.where(half == 0, flat[:16], flat[16:])
    slot_lengths = jnp.sum(
        jnp.where(cand_ids[:, None] == jnp.arange(16 * CAP_DP, dtype=jnp.int32)[None, :], lengths[None, :], 0), axis=1
    )

    attended = attend(order, slot, units, w_all, v_all, replies)

    my_lengths = jnp.where(half == 0, slot_lengths[:16], slot_lengths[16:])
    live = jnp.arange(L, dtype=jnp.int32)[None, :] < my_lengths[:, None]
    sums = jnp.sum(jnp.where(live, attended.reshape(2 * TOP, L), 0.0), axis=1)
    everyone = lax.all_to_all(
        jnp.broadcast_to(sums[None], (16, 2 * TOP)), TP, split_axis=0, concat_axis=0, tiled=True
    )
    pair_sum = jnp.sum(everyone.reshape(2, GROUPS, 2 * TOP), axis=1).reshape(IMG, TOP)
    pair_score = pair_sum / slot_lengths.reshape(IMG, TOP).astype(jnp.float32)
    slot_live = jnp.arange(TOP, dtype=jnp.int32)[None, :] < counts[:, None]
    return jnp.where(slot_live, pair_score, jnp.zeros_like(pair_score))


def solution(mesh):
    fine = Mesh(mesh.devices.reshape(4, 4, 4, 2, 2), ("zl", "x", "y", "zh", "c"))
    in_specs = (
        P(None, DP, TP),
        P(TP, None),
        P(TP, None),
        P(DP, None, None),
        P(DP),
        P(DP, None),
        P(DP),
    )
    return jax.shard_map(local, mesh=fine, in_specs=in_specs, out_specs=P(DP, None), check_vma=False)
```

time: 996 us -> 255 us (0.26)
  waiting for transfers between devices: 706 us -> 61 us
  other arithmetic: 83.2 us -> 7.66 us
  local copies, waits for them, and re-layouts: 97 us -> 31.4 us
  matrix products: 58.1 us -> 0 us
  Pallas kernels: 0 us -> 53.6 us
  starting transfers between devices: 13.7 us -> 55.7 us
  blocking collectives: 19.9 us -> 30.7 us
    all_gather x3 -> x1, waiting for transfers between devices: 271 us -> 0.01 us  [local(): w_all = lax.all_gather(w_mine, YC)]
    all_to_all x2 -> x4, waiting for transfers between devices: 240 us -> 15.5 us  [the longest x1 7.81 us: local(): lax.all_to_all(jnp.broadcast_to(sums[None], (16, 2 * TOP)), TP, split_axi...]
    reduce_scatter x2 -> x0, waiting for transfers between devices: 194 us -> none  [the longest x1 170 us: local(): lax.psum_scatter(jnp.dot(row_block, key_weight, preferred_element_type=jn...]
    add x30 -> x1, other arithmetic: 65.3 us -> 0.01 us  [local(): flat = (owners * 2 + own_rank).astype(jnp.int32)]
    dot_general x2 -> x0, matrix products: 57 us -> none  [the longest x1 45.9 us: local(): jnp.einsum('jklhd,pjhd->jkhlp', query_block, image_keys, precision=lax.Pr...]
    pallas_call x0 -> x2, Pallas kernels: none -> 53.6 us  [the longest x1 41.8 us: pick_queries(): pl.pallas_call(pick_kernel, out_shape=jax.ShapeDtypeStruct((2 * CAP_DP, L...]
    dynamic_slice x75 -> x1, local copies, waits for them, and re-layouts: 46.9 us -> 0.03 us  [local(): w_part = lax.dynamic_slice_in_dim(key_weight, part * rows, rows, axis=0)]
    ppermute x0 -> x19, waiting for transfers between devices: none -> 45.4 us  [the longest x3 35.1 us: flip(): return lax.ppermute(block, 'zl', [(i, i ^ mask) for i in range(4)])]
  transfers between devices with their start and end apart: 7 -> 24, of which waited for: 7 -> 10; matrix products, arithmetic and copies ran while one was open for 10% -> 10% of each run, Pallas kernels for 0% -> 16%
where the time goes in v1:
time: 255 us; the launch traced here: 254 us
  waiting for transfers between devices  61 us (24%)
  starting transfers between devices  55.7 us (22%)
  Pallas kernels  53.6 us (21%)
  local copies, waits for them, and re-layouts  31.4 us (12%)
  blocking collectives  30.7 us (12%)
  between operations  13.7 us (5%)
  other arithmetic  7.66 us (3%)
    pallas_call x1, Pallas kernels, pick_queries(): pl.pallas_call(pick_kernel, out_shape=jax.ShapeDtypeStruct((2 * CAP_DP, L...  41.8 us
    ppermute x3, waiting for transfers between devices, flip(): return lax.ppermute(block, 'zl', [(i, i ^ mask) for i in range(4)])  35.1 us
    all_to_all x1, blocking collectives, local(): w_mine = lax.all_to_all(w_sent, TP, split_axis=0, concat_axis=0, tiled=True)  30.7 us
    ppermute x16, starting transfers between devices, shift(): return lax.ppermute(block, axis, [(i, (i + by) % 4) for i in range(4)])  23.6 us
    unnamed x49, local copies, waits for them, and re-layouts  18.6 us
    pallas_call x1, Pallas kernels, attend(): pl.pallas_call(attend_kernel, out_shape=jax.ShapeDtypeStruct((2, TOP * L)...  11.8 us
    ppermute x16, waiting for transfers between devices, shift(): return lax.ppermute(block, axis, [(i, (i + by) % 4) for i in range(4)])  10.4 us
    all_to_all x1, starting transfers between devices, local(): lax.all_to_all(jnp.broadcast_to(sums[None], (16, 2 * TOP)), TP, split_axi...  9.14 us
  transfers between devices with their start and end apart: 24, of which 10 were waited for; matrix products, arithmetic and copies ran while one was open for 10% of the time, Pallas kernels for 16%

profile of v1, /device:TPU:8, one launch (start us, length us, event | category | flops | bytes accessed | tf_op | source)
XLA Modules:
  0.0 253.8 jit_solution(262312199075855303)
XLA Ops:
  6.5 1.9 copy-done
  8.8 30.7 %all_to_all.30 = bf16[16,40,640]{2,1,0:T(8,128)(2,1)} all-to-all(bf16[16,40,640]{2,1,0:T(8,128)(2,1)S(1)} %copy.33), channel_id=1, replica_groups=mesh['zl'=4,'x'=4,'y'=4,'zh'=2,'c'=2] {'zl','x'}, dimensions={0} | all-to-all | bytes 1638400 | tf_op jit(solution)/shard_map/all_to_all | solution.py:208
  40.3 8.9 %all-to-all-start = ((s32[16,1,48]{2,1,0:T(1,128)}), s32[16,1,48]{2,1,0:T(1,128)S(1)}, u32[]{:S(2)}, u32[]{:S(2)}) async-start(s32[16,1,48]{2,1,0:T(1,128)} %broadcast_in_dim.38), calls=%async_computation | async-start | bytes 16384 | tf_op jit(solution)/shard_map/all_to_all | solution.py:186
  49.3 0.7 pad_maximum_fusion.6
  49.9 7.7 %all-to-all-done = s32[16,1,48]{2,1,0:T(1,128)S(1)} async-done(((s32[16,1,48]{2,1,0:T(1,128)}), s32[16,1,48]{2,1,0:T(1,128)S(1)}, u32[]{:S(2)}, u32[]{:S(2)}) %all-to-all-start) | async-done | bytes 3104 | tf_op jit(solution)/shard_map/all_to_all | solution.py:186
  57.7 4.1 %all-to-all-start.2 = ((bf16[16,8,320]{2,1,0:T(8,128)(2,1)}), bf16[16,8,320]{2,1,0:T(8,128)(2,1)S(1)}, u32[]{:S(2)}, u32[]{:S(2)}) async-start(bf16[16,8,320]{2,1,0:T(8,128)(2,1)} %pad_maximum_fusion.6), calls=%async_computation.2 | async-start | bytes 196608 | tf_op jit(solution)/shard_map/all_to_all | solution.py:211
  62.4 0.6 reshape.131.ids
  63.0 41.8 %pick_queries.1 = bf16[32,32,640]{2,1,0:T(8,128)(2,1)} custom-call(s32[32]{0:T(128)} %reshape.131.ids, s32[1]{0:T(128)} %bitcast.27.col, bf16[16,32,5120]{2,1,0:T(8,128)(2,1)} %q_ref.1), custom_call_target="tpu_custom_call" | custom-call | bytes 2621440 | tf_op jit(solution)/shard_map/pick_queries/pallas_call | solution.py:42
  104.8 5.6 %all-to-all-start.3 = ((bf16[16,2,32,640]{3,2,1,0:T(8,128)(2,1)}), bf16[16,2,32,640]{3,2,1,0:T(8,128)(2,1)}, u32[]{:S(2)}, u32[]{:S(2)}) async-start(bf16[16,2,32,640]{3,2,1,0:T(8,128)(2,1)} %bitcast.39), calls=%async_computation.3 | async-start | bytes 2621440 | tf_op jit(solution)/shard_map/all_to_all | solution.py:226
  110.4 1.9 fusion.4
  112.3 1.8 copy.35
  114.1 1.8 copy.36
  115.9 1.5 fusion.5
  117.4 1.0 copy.37
  118.4 1.6 copy.38
  120.0 1.2 pad_maximum_fusion.1
  121.3 2.9 %collective-permute-start.9 = (bf16[256,640]{1,0:T(8,128)(2,1)S(1)}, bf16[256,640]{1,0:T(8,128)(2,1)}, u32[]{:S(2)}, u32[]{:S(2)}) collective-permute-start(bf16[256,640]{1,0:T(8,128)(2,1)S(1)} %get-tuple-element.7), channel_id=1, source_target_pairs={{0,128},{64,192},{128,0},{192,64},{1,129},{65,193},{129,1},{193,65... | collective-permute-start | bytes 983048 | tf_op jit(solution)/shard_map/ppermute | solution.py:164
  124.2 1.5 collective-permute-start.14
  125.6 1.5 collective-permute-start.1
  127.1 1.8 collective-permute-start
  128.9 0.7 copy-done.5
  129.8 35.1 %collective-permute-done.9.refs_8_ = bf16[256,640]{1,0:T(8,128)(2,1)} collective-permute-done((bf16[256,640]{1,0:T(8,128)(2,1)S(1)}, bf16[256,640]{1,0:T(8,128)(2,1)}, u32[]{:S(2)}, u32[]{:S(2)}) %collective-permute-start.9) | collective-permute-done | bytes 327712 | tf_op jit(solution)/shard_map/ppermute | solution.py:164
  164.9 1.5 collective-permute-start.11
  166.4 0.7 slice.89
  167.1 1.5 collective-permute-start.2
  168.6 1.8 collective-permute-start.10
  170.6 3.1 %collective-permute-start.15 = (bf16[256,640]{1,0:T(8,128)(2,1)}, bf16[256,640]{1,0:T(8,128)(2,1)}, u32[]{:S(2)}, u32[]{:S(2)}) collective-permute-start(bf16[256,640]{1,0:T(8,128)(2,1)} %collective-permute-done.14.refs_12_), channel_id=1, source_target_pairs={{0,48},{16,0},{32,16},{48,32},{1,49},{17,1},{33,17},{49,33},{2,50}... | collective-permute-start | bytes 983048 | tf_op jit(solution)/shard_map/ppermute | solution.py:160
  173.9 0.7 slice.82
  174.5 0.8 broadcast_in_dim.39
  175.3 1.7 collective-permute-done.11.refs_11_
  177.3 0.8 select_reduce_fusion
  178.1 0.9 slice.90
  179.0 0.9 slice.93
  180.0 3.0 %collective-permute-start.3 = (bf16[128,640]{1,0:T(8,128)(2,1)S(1)}, bf16[128,640]{1,0:T(8,128)(2,1)S(1)}, u32[]{:S(2)}, u32[]{:S(2)}) collective-permute-start(bf16[128,640]{1,0:T(8,128)(2,1)S(1)} %slice.90), channel_id=1, source_target_pairs={{0,48},{16,0},{32,16},{48,32},{1,49},{17,1},{33,17},{49,33},{2,50}... | collective-permute-start | bytes 491528 | tf_op jit(solution)/shard_map/ppermute | solution.py:160
  183.0 0.9 slice.94
  184.5 3.0 %collective-permute-done.16.refs_15_ = bf16[256,640]{1,0:T(8,128)(2,1)} collective-permute-done((bf16[256,640]{1,0:T(8,128)(2,1)}, bf16[256,640]{1,0:T(8,128)(2,1)}, u32[]{:S(2)}, u32[]{:S(2)}) %collective-permute-start.16) | collective-permute-done | bytes 327712 | tf_op jit(solution)/shard_map/ppermute | solution.py:160
  187.8 3.0 %collective-permute-start.13 = (bf16[128,640]{1,0:T(8,128)(2,1)S(1)}, bf16[128,640]{1,0:T(8,128)(2,1)S(1)}, u32[]{:S(2)}, u32[]{:S(2)}) collective-permute-start(bf16[128,640]{1,0:T(8,128)(2,1)S(1)} %slice.94), channel_id=1, source_target_pairs={{0,48},{16,0},{32,16},{48,32},{1,49},{17,1},{33,17},{49,33},{2,50}... | collective-permute-start | bytes 491528 | tf_op jit(solution)/shard_map/ppermute | solution.py:160
  190.8 0.9 slice.95
  191.8 0.9 slice.96
  192.8 1.6 collective-permute-done.6.refs_7_
  194.4 1.6 collective-permute-start.18
  196.0 0.8 pad_maximum_fusion.2.refs_2_
  197.0 1.2 collective-permute-start.7
  198.2 2.4 collective-permute-start.8
  200.6 0.8 pad_maximum_fusion.4.refs_10_
  201.5 2.6 %collective-permute-done.18 = bf16[128,640]{1,0:T(8,128)(2,1)S(1)} collective-permute-done((bf16[128,640]{1,0:T(8,128)(2,1)S(1)}, bf16[128,640]{1,0:T(8,128)(2,1)S(1)}, u32[]{:S(2)}, u32[]{:S(2)}) %collective-permute-start.18) | collective-permute-done | bytes 163872 | tf_op jit(solution)/shard_map/ppermute | solution.py:160
  204.0 0.8 pad_maximum_fusion.5.refs_14_
  204.8 1.1 collective-permute-done.8
  205.9 0.8 pad_maximum_fusion.3.refs_6_
  206.7 1.0 copy-done.1
  207.7 1.0 copy-done.2
  208.7 1.0 copy-done.3
  209.6 1.0 copy-done.4
  210.6 1.0 copy-done.6
  211.6 1.0 copy-done.8
  212.5 1.0 copy-done.10
  213.5 1.0 copy-done.12
  214.5 1.0 copy-done.14
  215.5 1.0 copy-done.16
  216.4 11.8 %attend.1 = f32[2,256]{1,0:T(2,128)S(1)} custom-call(s32[16]{0:T(128)S(1)} %stack.67.order, s32[16]{0:T(128)S(1)} %broadcast_select_fusion.slot, bf16[256,640]{1,0:T(8,128)(2,1)S(1)} %copy-done.6, bf16[256,640]{1,0:T(8,128)(2,1)S(1)} %copy-done.10, bf16[256,640]{1,0:T(8,128)(2,1)S(1)} %copy-done.1, bf16[256,640]{1,0:T(8,128)(2,1)S(1)} %copy-done.8, ...), custom_call_target="tpu_custom_call" | custom-call | flops 3355443200 | bytes 13631488 | tf_op jit(solution)/shard_map/attend/pallas_call | solution.py:134
  228.6 0.6 broadcast_in_dim.71
  229.2 9.1 %all-to-all-start.4 = ((f32[16,1,16]{2,1,0:T(1,128)}), f32[16,1,16]{2,1,0:T(1,128)S(1)}, u32[]{:S(2)}, u32[]{:S(2)}) async-start(f32[16,1,16]{2,1,0:T(1,128)} %broadcast_in_dim.71), calls=%async_computation.4 | async-start | bytes 16384 | tf_op jit(solution)/shard_map/all_to_all | solution.py:242
  238.4 7.8 %all-to-all-done.4 = f32[16,1,16]{2,1,0:T(1,128)S(1)} async-done(((f32[16,1,16]{2,1,0:T(1,128)}), f32[16,1,16]{2,1,0:T(1,128)S(1)}, u32[]{:S(2)}, u32[]{:S(2)}) %all-to-all-start.4) | async-done | bytes 1056 | tf_op jit(solution)/shard_map/all_to_all | solution.py:242
  246.3 0.6 divide_select_fusion
  (86 shorter events, 4.5 us)
Async XLA Ops:
  6.5 1.9 copy-start
  6.5 200.2 %all-gather.3.cloned.1.call-start = ((), (), s32[]{:S(2)}) async-start(), calls=%async_computation.5 | async-start | bytes 7372800 | tf_op jit(solution)/shard_map/all_gather | solution.py:209
  8.8 30.8 %copy-start.18 = (s32[4,8]{1,0:T(4,128)S(1)}, s32[4,8]{1,0:T(4,128)}, u32[]{:S(2)}) copy-start(s32[4,8]{1,0:T(4,128)} %param.12) | copy-start | bytes 388
  8.8 30.9 %copy-start.21 = (s32[16]{0:T(128)S(1)}, s32[16]{0:T(128)}, u32[]{:S(2)}) copy-start(s32[16]{0:T(128)} %param.11) | copy-start | bytes 196
  8.8 40.4 %copy-start.17 = (bf16[320,40]{0,1:T(8,128)(2,1)S(1)}, bf16[320,40]{0,1:T(8,128)(2,1)}, u32[]{:S(2)}) copy-start(bf16[320,40]{0,1:T(8,128)(2,1)} %param.9) | copy-start | bytes 76804
  39.7 126.7 %copy-start.19 = (s32[32]{0:T(128)}, s32[32]{0:T(128)S(1)}, u32[]{:S(2)}) copy-start(s32[32]{0:T(128)S(1)} %eq.74) | copy-start | bytes 388
  40.3 17.3 %all-to-all-start = ((s32[16,1,48]{2,1,0:T(1,128)}), s32[16,1,48]{2,1,0:T(1,128)S(1)}, u32[]{:S(2)}, u32[]{:S(2)}) async-start(s32[16,1,48]{2,1,0:T(1,128)} %broadcast_in_dim.38), calls=%async_computation | async-start | bytes 16384 | tf_op jit(solution)/shard_map/all_to_all | solution.py:186
  57.7 47.1 %all-to-all-start.2 = ((bf16[16,8,320]{2,1,0:T(8,128)(2,1)}), bf16[16,8,320]{2,1,0:T(8,128)(2,1)S(1)}, u32[]{:S(2)}, u32[]{:S(2)}) async-start(bf16[16,8,320]{2,1,0:T(8,128)(2,1)} %pad_maximum_fusion.6), calls=%async_computation.2 | async-start | bytes 196608 | tf_op jit(solution)/shard_map/all_to_all | solution.py:211
  104.8 101.9 %all-to-all-start.3 = ((bf16[16,2,32,640]{3,2,1,0:T(8,128)(2,1)}), bf16[16,2,32,640]{3,2,1,0:T(8,128)(2,1)}, u32[]{:S(2)}, u32[]{:S(2)}) async-start(bf16[16,2,32,640]{3,2,1,0:T(8,128)(2,1)} %bitcast.39), calls=%async_computation.3 | async-start | bytes 2621440 | tf_op jit(solution)/shard_map/all_to_all | solution.py:226
  121.3 43.6 %collective-permute-start.9 = (bf16[256,640]{1,0:T(8,128)(2,1)S(1)}, bf16[256,640]{1,0:T(8,128)(2,1)}, u32[]{:S(2)}, u32[]{:S(2)}) collective-permute-start(bf16[256,640]{1,0:T(8,128)(2,1)S(1)} %get-tuple-element.7), channel_id=1, source_target_pairs={{0,128},{64,192},{128,0},{192,64},{1,129},{65,193},{129,1},{193,65... | collective-permute-start | bytes 983048 | tf_op jit(solution)/shard_map/ppermute | solution.py:164
  124.2 44.4 %collective-permute-start.14 = (bf16[256,640]{1,0:T(8,128)(2,1)S(1)}, bf16[256,640]{1,0:T(8,128)(2,1)}, u32[]{:S(2)}, u32[]{:S(2)}) collective-permute-start(bf16[256,640]{1,0:T(8,128)(2,1)S(1)} %get-tuple-element.7), channel_id=1, source_target_pairs={{0,192},{64,128},{128,64},{192,0},{1,193},{65,129},{129,65},{193,1... | collective-permute-start | bytes 983048 | tf_op jit(solution)/shard_map/ppermute | solution.py:164
  125.6 44.7 %collective-permute-start.4 = (bf16[256,640]{1,0:T(8,128)(2,1)S(1)}, bf16[256,640]{1,0:T(8,128)(2,1)S(1)}, u32[]{:S(2)}, u32[]{:S(2)}) collective-permute-start(bf16[256,640]{1,0:T(8,128)(2,1)S(1)} %get-tuple-element.8.refs_0_), channel_id=1, source_target_pairs={{0,64},{64,0},{128,192},{192,128},{1,65},{65,1},{129,193},{193,129... | collective-permute-start | bytes 983048 | tf_op jit(solution)/shard_map/ppermute | solution.py:164
  125.6 40.8 %collective-permute-start.1 = (bf16[256,640]{1,0:T(8,128)(2,1)S(1)}, bf16[256,640]{1,0:T(8,128)(2,1)S(1)}, u32[]{:S(2)}, u32[]{:S(2)}) collective-permute-start(bf16[256,640]{1,0:T(8,128)(2,1)S(1)} %get-tuple-element.8.refs_0_), channel_id=1, source_target_pairs={{0,16},{16,32},{32,48},{48,0},{1,17},{17,33},{33,49},{49,1},{2,18}... | collective-permute-start | bytes 983048 | tf_op jit(solution)/shard_map/ppermute | solution.py:160
  127.1 43.5 %collective-permute-start = (bf16[256,640]{1,0:T(8,128)(2,1)S(1)}, bf16[256,640]{1,0:T(8,128)(2,1)S(1)}, u32[]{:S(2)}, u32[]{:S(2)}) collective-permute-start(bf16[256,640]{1,0:T(8,128)(2,1)S(1)} %get-tuple-element.8.refs_0_), channel_id=1, source_target_pairs={{0,48},{16,0},{32,16},{48,32},{1,49},{17,1},{33,17},{49,33},{2,50}... | collective-permute-start | bytes 983048 | tf_op jit(solution)/shard_map/ppermute | solution.py:160
  128.9 0.7 copy-start.5
  164.9 12.1 %collective-permute-start.11 = (bf16[256,640]{1,0:T(8,128)(2,1)}, bf16[256,640]{1,0:T(8,128)(2,1)}, u32[]{:S(2)}, u32[]{:S(2)}) collective-permute-start(bf16[256,640]{1,0:T(8,128)(2,1)} %collective-permute-done.9.refs_8_), channel_id=1, source_target_pairs={{0,16},{16,32},{32,48},{48,0},{1,17},{17,33},{33,49},{49,1},{2,18}... | collective-permute-start | bytes 983048 | tf_op jit(solution)/shard_map/ppermute | solution.py:160
  166.4 4.2 %copy-start.7 = (bf16[256,640]{1,0:T(8,128)(2,1)}, bf16[256,640]{1,0:T(8,128)(2,1)S(1)}, u32[]{:S(2)}) copy-start(bf16[256,640]{1,0:T(8,128)(2,1)S(1)} %collective-permute-done.1.refs_3_) | copy-start | bytes 983044
  167.1 16.8 %collective-permute-start.2 = (bf16[128,640]{1,0:T(8,128)(2,1)}, bf16[128,640]{1,0:T(8,128)(2,1)S(1)}, u32[]{:S(2)}, u32[]{:S(2)}) collective-permute-start(bf16[128,640]{1,0:T(8,128)(2,1)} %slice.89), channel_id=1, source_target_pairs={{0,16},{16,32},{32,48},{48,0},{1,17},{17,33},{33,49},{49,1},{2,18}... | collective-permute-start | bytes 491528 | tf_op jit(solution)/shard_map/ppermute | solution.py:160
  168.6 11.4 %collective-permute-start.10 = (bf16[256,640]{1,0:T(8,128)(2,1)}, bf16[256,640]{1,0:T(8,128)(2,1)}, u32[]{:S(2)}, u32[]{:S(2)}) collective-permute-start(bf16[256,640]{1,0:T(8,128)(2,1)} %collective-permute-done.9.refs_8_), channel_id=1, source_target_pairs={{0,48},{16,0},{32,16},{48,32},{1,49},{17,1},{33,17},{49,33},{2,50}... | collective-permute-start | bytes 983048 | tf_op jit(solution)/shard_map/ppermute | solution.py:160
  170.4 3.3 %copy-start.15 = (bf16[256,640]{1,0:T(8,128)(2,1)}, bf16[256,640]{1,0:T(8,128)(2,1)S(1)}, u32[]{:S(2)}) copy-start(bf16[256,640]{1,0:T(8,128)(2,1)S(1)} %collective-permute-done.4.refs_4_) | copy-start | bytes 983044
  170.4 17.1 %collective-permute-start.16 = (bf16[256,640]{1,0:T(8,128)(2,1)}, bf16[256,640]{1,0:T(8,128)(2,1)}, u32[]{:S(2)}, u32[]{:S(2)}) collective-permute-start(bf16[256,640]{1,0:T(8,128)(2,1)} %collective-permute-done.14.refs_12_), channel_id=1, source_target_pairs={{0,16},{16,32},{32,48},{48,0},{1,17},{17,33},{33,49},{49,1},{2,18}... | collective-permute-start | bytes 983048 | tf_op jit(solution)/shard_map/ppermute | solution.py:160
  170.6 3.1 %copy-start.9 = (bf16[256,640]{1,0:T(8,128)(2,1)}, bf16[256,640]{1,0:T(8,128)(2,1)S(1)}, u32[]{:S(2)}) copy-start(bf16[256,640]{1,0:T(8,128)(2,1)S(1)} %collective-permute-done.refs_1_) | copy-start | bytes 983044
  170.6 17.2 %collective-permute-start.15 = (bf16[256,640]{1,0:T(8,128)(2,1)}, bf16[256,640]{1,0:T(8,128)(2,1)}, u32[]{:S(2)}, u32[]{:S(2)}) collective-permute-start(bf16[256,640]{1,0:T(8,128)(2,1)} %collective-permute-done.14.refs_12_), channel_id=1, source_target_pairs={{0,48},{16,0},{32,16},{48,32},{1,49},{17,1},{33,17},{49,33},{2,50}... | collective-permute-start | bytes 983048 | tf_op jit(solution)/shard_map/ppermute | solution.py:160
  177.0 17.4 %collective-permute-start.6 = (bf16[256,640]{1,0:T(8,128)(2,1)}, bf16[256,640]{1,0:T(8,128)(2,1)S(1)}, u32[]{:S(2)}, u32[]{:S(2)}) collective-permute-start(bf16[256,640]{1,0:T(8,128)(2,1)} %copy-done.15), channel_id=1, source_target_pairs={{0,16},{16,32},{32,48},{48,0},{1,17},{17,33},{33,49},{49,1},{2,18}... | collective-permute-start | bytes 983048 | tf_op jit(solution)/shard_map/ppermute | solution.py:160
  180.0 12.7 %collective-permute-start.3 = (bf16[128,640]{1,0:T(8,128)(2,1)S(1)}, bf16[128,640]{1,0:T(8,128)(2,1)S(1)}, u32[]{:S(2)}, u32[]{:S(2)}) collective-permute-start(bf16[128,640]{1,0:T(8,128)(2,1)S(1)} %slice.90), channel_id=1, source_target_pairs={{0,48},{16,0},{32,16},{48,32},{1,49},{17,1},{33,17},{49,33},{2,50}... | collective-permute-start | bytes 491528 | tf_op jit(solution)/shard_map/ppermute | solution.py:160
  184.0 13.0 %collective-permute-start.5 = (bf16[256,640]{1,0:T(8,128)(2,1)}, bf16[256,640]{1,0:T(8,128)(2,1)S(1)}, u32[]{:S(2)}, u32[]{:S(2)}) collective-permute-start(bf16[256,640]{1,0:T(8,128)(2,1)} %copy-done.15), channel_id=1, source_target_pairs={{0,48},{16,0},{32,16},{48,32},{1,49},{17,1},{33,17},{49,33},{2,50}... | collective-permute-start | bytes 983048 | tf_op jit(solution)/shard_map/ppermute | solution.py:160
  187.5 10.7 %collective-permute-start.12 = (bf16[128,640]{1,0:T(8,128)(2,1)S(1)}, bf16[128,640]{1,0:T(8,128)(2,1)S(1)}, u32[]{:S(2)}, u32[]{:S(2)}) collective-permute-start(bf16[128,640]{1,0:T(8,128)(2,1)S(1)} %slice.93), channel_id=1, source_target_pairs={{0,16},{16,32},{32,48},{48,0},{1,17},{17,33},{33,49},{49,1},{2,18}... | collective-permute-start | bytes 491528 | tf_op jit(solution)/shard_map/ppermute | solution.py:160
  187.8 12.8 %collective-permute-start.13 = (bf16[128,640]{1,0:T(8,128)(2,1)S(1)}, bf16[128,640]{1,0:T(8,128)(2,1)S(1)}, u32[]{:S(2)}, u32[]{:S(2)}) collective-permute-start(bf16[128,640]{1,0:T(8,128)(2,1)S(1)} %slice.94), channel_id=1, source_target_pairs={{0,48},{16,0},{32,16},{48,32},{1,49},{17,1},{33,17},{49,33},{2,50}... | collective-permute-start | bytes 491528 | tf_op jit(solution)/shard_map/ppermute | solution.py:160
  192.7 8.7 %collective-permute-start.17 = (bf16[128,640]{1,0:T(8,128)(2,1)S(1)}, bf16[128,640]{1,0:T(8,128)(2,1)S(1)}, u32[]{:S(2)}, u32[]{:S(2)}) collective-permute-start(bf16[128,640]{1,0:T(8,128)(2,1)S(1)} %slice.95), channel_id=1, source_target_pairs={{0,16},{16,32},{32,48},{48,0},{1,17},{17,33},{33,49},{49,1},{2,18}... | collective-permute-start | bytes 491528 | tf_op jit(solution)/shard_map/ppermute | solution.py:160
  194.4 10.3 %copy-start.11 = (bf16[256,640]{1,0:T(8,128)(2,1)}, bf16[256,640]{1,0:T(8,128)(2,1)S(1)}, u32[]{:S(2)}) copy-start(bf16[256,640]{1,0:T(8,128)(2,1)S(1)} %collective-permute-done.6.refs_7_) | copy-start | bytes 983044
  194.4 9.6 %collective-permute-start.18 = (bf16[128,640]{1,0:T(8,128)(2,1)S(1)}, bf16[128,640]{1,0:T(8,128)(2,1)S(1)}, u32[]{:S(2)}, u32[]{:S(2)}) collective-permute-start(bf16[128,640]{1,0:T(8,128)(2,1)S(1)} %slice.96), channel_id=1, source_target_pairs={{0,48},{16,0},{32,16},{48,32},{1,49},{17,1},{33,17},{49,33},{2,50}... | collective-permute-start | bytes 491528 | tf_op jit(solution)/shard_map/ppermute | solution.py:160
  197.0 7.8 %copy-start.13 = (bf16[256,640]{1,0:T(8,128)(2,1)}, bf16[256,640]{1,0:T(8,128)(2,1)S(1)}, u32[]{:S(2)}) copy-start(bf16[256,640]{1,0:T(8,128)(2,1)S(1)} %collective-permute-done.5.refs_5_) | copy-start | bytes 983044
  197.0 7.8 %collective-permute-start.7 = (bf16[128,640]{1,0:T(8,128)(2,1)S(1)}, bf16[128,640]{1,0:T(8,128)(2,1)S(1)}, u32[]{:S(2)}, u32[]{:S(2)}) collective-permute-start(bf16[128,640]{1,0:T(8,128)(2,1)S(1)} %slice.91), channel_id=1, source_target_pairs={{0,16},{16,32},{32,48},{48,0},{1,17},{17,33},{33,49},{49,1},{2,18}... | collective-permute-start | bytes 491528 | tf_op jit(solution)/shard_map/ppermute | solution.py:160
  198.2 7.7 %collective-permute-start.8 = (bf16[128,640]{1,0:T(8,128)(2,1)S(1)}, bf16[128,640]{1,0:T(8,128)(2,1)S(1)}, u32[]{:S(2)}, u32[]{:S(2)}) collective-permute-start(bf16[128,640]{1,0:T(8,128)(2,1)S(1)} %slice.92), channel_id=1, source_target_pairs={{0,48},{16,0},{32,16},{48,32},{1,49},{17,1},{33,17},{49,33},{2,50}... | collective-permute-start | bytes 491528 | tf_op jit(solution)/shard_map/ppermute | solution.py:160
  206.7 1.0 copy-start.1
  207.7 1.0 copy-start.2
  208.6 1.0 copy-start.3
  209.6 1.0 copy-start.4
  210.6 1.0 copy-start.6
  211.6 1.0 copy-start.8
  212.5 1.0 copy-start.10
  213.5 1.0 copy-start.12
  214.5 1.0 copy-start.14
  215.5 1.0 copy-start.16
  216.4 29.9 %copy-start.20 = (s32[4]{0:T(128)S(1)}, s32[4]{0:T(128)}, u32[]{:S(2)}) copy-start(s32[4]{0:T(128)} %param.13) | copy-start | bytes 52
  229.2 17.0 %all-to-all-start.4 = ((f32[16,1,16]{2,1,0:T(1,128)}), f32[16,1,16]{2,1,0:T(1,128)S(1)}, u32[]{:S(2)}, u32[]{:S(2)}) async-start(f32[16,1,16]{2,1,0:T(1,128)} %broadcast_in_dim.71), calls=%async_computation.4 | async-start | bytes 16384 | tf_op jit(solution)/shard_map/all_to_all | solution.py:242
Sparse Core Ops, SparseCore 0:
  39.7 42.5 all-gather.2

commit v2 on v1

v2 whole, which is shorter than its diff:
```python
import functools

import jax
import jax.numpy as jnp
from jax import lax
from jax.experimental import pallas as pl
from jax.experimental.pallas import tpu as pltpu
from jax.sharding import Mesh
from jax.sharding import PartitionSpec as P

H = 40
HD = 128
L = 32
TOP = 8
CAP_DP = 16
IMG = 4
GROUPS = 8
GH = H // GROUPS
GW = GH * HD
PATCH = 256
FEAT = 320
TP = ("zl", "x")
DP = ("y", "zh", "c")
YC = ("y", "c")


def pick_kernel(ids, col, q_ref, o_ref, sem):
    copies = []
    for r in range(2 * CAP_DP):
        start = pl.multiple_of(col[r] * GW, 128)
        copies.append(
            pltpu.make_async_copy(q_ref.at[ids[r], :, pl.ds(start, GW)], o_ref.at[r], sem.at[r])
        )
    for c in copies:
        c.start()
    for c in copies:
        c.wait()


def pick_queries(queries, ids, col):
    return pl.pallas_call(
        pick_kernel,
        out_shape=jax.ShapeDtypeStruct((2 * CAP_DP, L, GW), queries.dtype),
        in_specs=[
            pl.BlockSpec(memory_space=pltpu.SMEM),
            pl.BlockSpec(memory_space=pltpu.SMEM),
            pl.BlockSpec(memory_space=pltpu.HBM),
        ],
        out_specs=pl.BlockSpec(memory_space=pltpu.VMEM),
        scratch_shapes=[pltpu.SemaphoreType.DMA((2 * CAP_DP,))],
        compiler_params=pltpu.CompilerParams(vmem_limit_bytes=8 * 2**20),
        cost_estimate=pl.CostEstimate(flops=10**11, bytes_accessed=3 * 10**8, transcendentals=0),
        name="pick_queries",
    )(ids, col, queries)


def attend_kernel(order, slot, *refs):
    units = refs[:16]
    w_ref, v_ref, near_ref, far_ref, o_ref = refs[16:21]
    ws, q_ref, acc, val, wsem = refs[21:]
    wcopy = [pltpu.make_async_copy(w_ref.at[:, order[u]], ws.at[u], wsem.at[u]) for u in range(16)]
    for u in range(16):
        wcopy[u].start()

    for step in range(8):
        some = range(2 * step, 2 * step + 2)
        for u in some:
            wcopy[u].wait()
        w = jnp.concatenate(
            [ws[u].astype(jnp.float32).reshape(FEAT, GW).astype(jnp.bfloat16) for u in some], axis=0
        )
        v = jnp.concatenate([v_ref[order[u]] for u in some], axis=1)
        for i in range(2):
            x = jnp.concatenate([units[u][i] for u in some], axis=0)
            keys = lax.dot_general(
                x, w, (((0,), (0,)), ((), ())), preferred_element_type=jnp.float32
            )
            values = jnp.dot(v, x, preferred_element_type=jnp.float32)
            if step == 0:
                acc[i] = keys
                val[i] = values
            else:
                acc[i] += keys
                val[i] += values
    q_ref[0:CAP_DP] = near_ref[...]
    q_ref[CAP_DP:] = far_ref[...]
    scale = float(HD) ** (-0.5)
    part = functools.partial(
        lax.dot_general,
        dimension_numbers=(((1,), (1,)), ((), ())),
        preferred_element_type=jnp.float32,
    )
    for i in range(2):
        q = jnp.concatenate([q_ref[slot[TOP * i + k]] for k in range(TOP)], axis=0)
        v_all = val[i].T
        total = jnp.zeros((1, TOP * L), jnp.float32)
        for h in range(GH):
            k = acc[i, :, HD * h : HD * (h + 1)]
            qh = q[:, HD * h : HD * (h + 1)]
            k1 = k.astype(jnp.bfloat16)
            r1 = k - k1.astype(jnp.float32)
            k2 = r1.astype(jnp.bfloat16)
            k3 = (r1 - k2.astype(jnp.float32)).astype(jnp.bfloat16)
            logits = (part(k3, qh) + part(k2, qh) + part(k1, qh)) * scale
            peak = jnp.max(logits, axis=0, keepdims=True)
            e = jnp.exp(logits - peak)
            norm = jnp.sum(e, axis=0, keepdims=True)
            total = total + jnp.sum(e * v_all[:, h : h + 1], axis=0, keepdims=True) / norm
        o_ref[i : i + 1, :] = total


def attend(order, slot, units, w, v, near, far):
    vmem = pl.BlockSpec(memory_space=pltpu.VMEM)
    return pl.pallas_call(
        attend_kernel,
        out_shape=jax.ShapeDtypeStruct((2, TOP * L), jnp.float32),
        in_specs=[pl.BlockSpec(memory_space=pltpu.SMEM)] * 2
        + [vmem] * 16
        + [pl.BlockSpec(memory_space=pltpu.HBM)] + [vmem] * 3,
        out_specs=vmem,
        scratch_shapes=[
            pltpu.VMEM((16, GROUPS, FEAT // 8, GW), jnp.bfloat16),
            pltpu.VMEM((2 * CAP_DP, L, GW), jnp.bfloat16),
            pltpu.VMEM((2, PATCH, GW), jnp.float32),
            pltpu.VMEM((2, 8, PATCH), jnp.float32),
            pltpu.SemaphoreType.DMA((16,)),
        ],
        compiler_params=pltpu.CompilerParams(vmem_limit_bytes=52 * 2**20),
        cost_estimate=pl.CostEstimate(
            flops=2 * 512 * 5120 * 640, bytes_accessed=13 * 2**20, transcendentals=655360
        ),
        name="attend",
    )(order, slot, *units, w, v, near, far)


def mark_kernel(x_ref, o_ref):
    o_ref[...] = x_ref[...]


def mark(token, *held):
    token, *held = lax.optimization_barrier((token, *held))
    token = pl.pallas_call(
        mark_kernel,
        out_shape=jax.ShapeDtypeStruct(token.shape, token.dtype),
        in_specs=[pl.BlockSpec(memory_space=pltpu.VMEM)],
        out_specs=pl.BlockSpec(memory_space=pltpu.VMEM),
        compiler_params=pltpu.CompilerParams(vmem_limit_bytes=2**20),
        cost_estimate=pl.CostEstimate(flops=10**11, bytes_accessed=3 * 10**8, transcendentals=0),
        name="mark",
    )(token)
    return token, *held


def shift(block, axis, by):
    return lax.ppermute(block, axis, [(i, (i + by) % 4) for i in range(4)])


def flip(block, mask):
    return lax.ppermute(block, "zl", [(i, i ^ mask) for i in range(4)])


def ring(unit):
    return [unit, shift(unit, "x", -1), shift(unit, "x", 2), shift(unit, "x", 1)]


def local(img_tokens, key_weight, value_map, queries, cap_lengths, candidates, counts):
    zl, x, zh = lax.axis_index("zl"), lax.axis_index("x"), lax.axis_index("zh")
    half = zl // 2
    group = (zl % 2) * 4 + x
    me = lax.axis_index(DP)
    part = lax.axis_index(YC)

    rows = FEAT // 8
    w_part = lax.dynamic_slice_in_dim(key_weight, part * rows, rows, axis=0)
    w_part = jnp.swapaxes(w_part.reshape(rows, GROUPS, GW), 0, 1)
    v_part = jnp.pad(value_map.T.reshape(GROUPS, GH, FEAT), ((0, 0), (0, 8 - GH), (0, GW - FEAT)))
    w_part = jnp.concatenate([w_part, v_part], axis=1)
    w_sent = jnp.concatenate([w_part, w_part], axis=0)

    tokens = jnp.transpose(img_tokens, (1, 2, 0))
    mine = lax.dynamic_slice_in_dim(tokens, 2 * half, 2, axis=0)
    theirs = lax.dynamic_slice_in_dim(tokens, 2 - 2 * half, 2, axis=0)
    over = flip(theirs, 2)
    beside = flip(mine, 1)
    own = ring(mine)
    order = jnp.stack([(zl ^ d) * 4 + (x + e) % 4 for d in range(4) for e in range(4)]).astype(jnp.int32)

    slot_total = IMG * TOP
    cand_ids = candidates.reshape(slot_total)
    notice = jnp.broadcast_to(jnp.concatenate([cand_ids, cap_lengths])[None], (16, slot_total + CAP_DP))
    notice, mine, theirs = mark(notice, mine, theirs)
    notices = lax.all_to_all(notice, DP, split_axis=0, concat_axis=0, tiled=True)
    w_mine = lax.all_to_all(w_sent, TP, split_axis=0, concat_axis=0, tiled=True)
    w_mine, img_tokens = lax.optimization_barrier((w_mine, img_tokens))
    w_all = lax.all_gather(w_mine[:, :rows], YC)
    v_all = w_mine[:, rows:, :FEAT]

    notices, own, beside, over = lax.optimization_barrier((notices, own, beside, over))
    last = flip(over, 1)
    beside, over = ring(beside), ring(over)
    notices, last, *beside = mark(notices, last, *beside)

    asked = notices[:, :slot_total]
    lengths = notices[:, slot_total:].reshape(16 * CAP_DP)
    match = (asked // CAP_DP) == me
    slots = jnp.arange(slot_total, dtype=jnp.int32)
    earlier = slots[:, None] > slots[None, :]
    rank = jnp.sum((match[:, None, :] & earlier[None]).astype(jnp.int32), axis=2)
    ids = jnp.sum(
        jnp.where(match[:, None, :] & (rank[:, None, :] == jnp.arange(2)[None, :, None]), asked[:, None, :] % CAP_DP, 0),
        axis=2,
    ).reshape(2 * CAP_DP)
    same = (jnp.arange(2 * CAP_DP, dtype=jnp.int32) // 4) % 2 == zh
    columns = jnp.where(same, group, (1 - zl % 2) * 4 + x)
    picked = pick_queries(queries, ids.astype(jnp.int32), columns.astype(jnp.int32))
    picked = picked.reshape(4, 2, 2, 2, L, GW)
    near = lax.dynamic_index_in_dim(picked, zh, axis=1, keepdims=False)
    far = lax.dynamic_index_in_dim(picked, 1 - zh, axis=1, keepdims=False)
    far = lax.ppermute(far, ("zl", "zh"), [(2 * a + b, 2 * (3 - a) + 1 - b) for a in range(4) for b in range(2)])
    near = lax.all_to_all(near.reshape(8, 2, L, GW), YC, split_axis=0, concat_axis=0, tiled=True)
    last = ring(last)
    far, near, last, over = lax.optimization_barrier((far, near, last, over))
    far = lax.all_to_all(far.reshape(8, 2, L, GW), YC, split_axis=0, concat_axis=0, tiled=True)
    units = own + beside + over + last
    near = near.reshape(CAP_DP, L, GW)
    far = far.reshape(CAP_DP, L, GW)
    owners = cand_ids // CAP_DP
    own_rank = jnp.sum(((owners[:, None] == owners[None, :]) & earlier).astype(jnp.int32), axis=1)
    owner_zh = (owners // 2) % 2
    place = (owners // 4) * 2 + owners % 2
    flat = ((owner_zh ^ zh) * CAP_DP + place * 2 + own_rank).astype(jnp.int32)
    slot = jnp.where(half == 0, flat[:16], flat[16:])
    slot_lengths = jnp.sum(
        jnp.where(cand_ids[:, None] == jnp.arange(16 * CAP_DP, dtype=jnp.int32)[None, :], lengths[None, :], 0), axis=1
    )

    attended = attend(order, slot, units, w_all, v_all, near, far)

    my_lengths = jnp.where(half == 0, slot_lengths[:16], slot_lengths[16:])
    live = jnp.arange(L, dtype=jnp.int32)[None, :] < my_lengths[:, None]
    sums = jnp.sum(jnp.where(live, attended.reshape(2 * TOP, L), 0.0), axis=1)
    everyone = lax.all_to_all(
        jnp.broadcast_to(sums[None], (16, 2 * TOP)), TP, split_axis=0, concat_axis=0, tiled=True
    )
    pair_sum = jnp.sum(everyone.reshape(2, GROUPS, 2 * TOP), axis=1).reshape(IMG, TOP)
    pair_score = pair_sum / slot_lengths.reshape(IMG, TOP).astype(jnp.float32)
    slot_live = jnp.arange(TOP, dtype=jnp.int32)[None, :] < counts[:, None]
    return jnp.where(slot_live, pair_score, jnp.zeros_like(pair_score))


def solution(mesh):
    fine = Mesh(mesh.devices.reshape(4, 4, 4, 2, 2), ("zl", "x", "y", "zh", "c"))
    in_specs = (
        P(None, DP, TP),
        P(TP, None),
        P(TP, None),
        P(DP, None, None),
        P(DP),
        P(DP, None),
        P(DP),
    )
    return jax.shard_map(local, mesh=fine, in_specs=in_specs, out_specs=P(DP, None), check_vma=False)
```

time: 255 us -> 167 us (0.65)
  Pallas kernels: 53.6 us -> 14.7 us
  blocking collectives: 30.7 us -> 0 us
  local copies, waits for them, and re-layouts: 31.4 us -> 14.3 us
  other arithmetic: 7.66 us -> 4.19 us
  waiting for transfers between devices: 61 us -> 64 us
    pallas_call x1, Pallas kernels: 41.8 us -> 1.43 us  [pick_queries(): pl.pallas_call(pick_kernel, out_shape=jax.ShapeDtypeStruct((2 * CAP_DP, L...]
    ppermute x3, waiting for transfers between devices: 35.1 us -> 0.01 us  [flip(): return lax.ppermute(block, 'zl', [(i, i ^ mask) for i in range(4)])]
    all_to_all x1 -> x0, blocking collectives: 30.7 us -> none  [local(): w_mine = lax.all_to_all(w_sent, TP, split_axis=0, concat_axis=0, tiled=True)]
    ppermute x16 -> x12, waiting for transfers between devices: 10.4 us -> 40.3 us  [shift(): return lax.ppermute(block, axis, [(i, (i + by) % 4) for i in range(4)])]
    unnamed x49 -> x22, local copies, waits for them, and re-layouts: 18.6 us -> 4.05 us
    all_to_all x2 -> x3, waiting for transfers between devices: 0.01 us -> 10.4 us  [the longest x1 10.4 us: local(): lax.all_to_all(far.reshape(8, 2, L, GW), YC, split_axis=0, concat_axis=0,...]
    ppermute x16 -> x12, starting transfers between devices: 23.6 us -> 16.9 us  [shift(): return lax.ppermute(block, axis, [(i, (i + by) % 4) for i in range(4)])]
    slice x10 -> x2, local copies, waits for them, and re-layouts: 8.8 us -> 3.11 us  [the longest x1 2.19 us: local(): w_all = lax.all_gather(w_mine[:, :rows], YC)]
  transfers between devices with their start and end apart: 24 -> 22, of which waited for: 10 -> 8; matrix products, arithmetic and copies ran while one was open for 10% -> 6% of each run, Pallas kernels for 16% -> 1%
where the time goes in v2:
time: 167 us
  waiting for transfers between devices  64 us (38%)
  starting transfers between devices  55.8 us (33%)
  Pallas kernels  14.7 us (9%)
  local copies, waits for them, and re-layouts  14.3 us (9%)
  between operations  13.7 us (8%)
  other arithmetic  4.19 us (3%)
    ppermute x12, waiting for transfers between devices, shift(): return lax.ppermute(block, axis, [(i, (i + by) % 4) for i in range(4)])  40.3 us
    ppermute x12, starting transfers between devices, shift(): return lax.ppermute(block, axis, [(i, (i + by) % 4) for i in range(4)])  16.9 us
    pallas_call x1, Pallas kernels, attend(): pl.pallas_call(attend_kernel, out_shape=jax.ShapeDtypeStruct((2, TOP * L)...  12.6 us
    all_to_all x1, waiting for transfers between devices, local(): lax.all_to_all(far.reshape(8, 2, L, GW), YC, split_axis=0, concat_axis=0,...  10.4 us
    all_to_all x1, starting transfers between devices, local(): lax.all_to_all(notice, DP, split_axis=0, concat_axis=0, tiled=True)  8.86 us
    all_to_all x1, waiting for transfers between devices, local(): lax.all_to_all(jnp.broadcast_to(sums[None], (16, 2 * TOP)), TP, split_axi...  7.82 us
    all_to_all x1, starting transfers between devices, local(): lax.all_to_all(jnp.broadcast_to(sums[None], (16, 2 * TOP)), TP, split_axi...  7.32 us
    ppermute x3, starting transfers between devices, flip(): return lax.ppermute(block, 'zl', [(i, i ^ mask) for i in range(4)])  6.68 us
  transfers between devices with their start and end apart: 22, of which 8 were waited for; matrix products, arithmetic and copies ran while one was open for 6% of the time, Pallas kernels for 1%

profile of v2, /device:TPU:8, one launch (start us, length us, event | category | flops | bytes accessed | tf_op | source)
XLA Modules:
  0.0 166.7 jit_solution(1906104452308284405)
XLA Ops:
  6.5 2.1 %dynamic-slice_bitcast_fusion.1 = (bf16[2,320,256]{2,1,0:T(8,128)(2,1)}, bf16[2,320,256]{2,1,0:T(8,128)(2,1)}) fusion(bf16[256,4,320]{0,2,1:T(8,128)(2,1)} %param.7, s32[]{:T(128)S(6)} %select_n.152, s32[]{:T(128)S(6)} %select_n.151), kind=kLoop, calls=%fused_computation.3 | loop fusion | bytes 1310728 | tf_op jit(solution)/shard_map/dynamic_slice | solution.py:182
  8.6 1.9 %collective-permute-start.3 = (bf16[2,320,256]{2,1,0:T(8,128)(2,1)}, bf16[2,320,256]{2,1,0:T(8,128)(2,1)}, u32[]{:S(2)}, u32[]{:S(2)}) collective-permute-start(bf16[2,320,256]{2,1,0:T(8,128)(2,1)} %get-tuple-element.35.refs_0_), channel_id=1, source_target_pairs={{0,64},{64,0},{128,192},{192,128},{1,65},{65,1},{129,193},{193,129... | collective-permute-start | bytes 983048 | tf_op jit(solution)/shard_map/ppermute | solution.py:159
  10.6 1.5 collective-permute-start.2
  12.1 2.7 %collective-permute-start.1 = (bf16[2,320,256]{2,1,0:T(8,128)(2,1)}, bf16[2,320,256]{2,1,0:T(8,128)(2,1)}, u32[]{:S(2)}, u32[]{:S(2)}) collective-permute-start(bf16[2,320,256]{2,1,0:T(8,128)(2,1)} %get-tuple-element.35.refs_0_), channel_id=1, source_target_pairs={{0,32},{16,48},{32,0},{48,16},{1,33},{17,49},{33,1},{49,17},{2,34}... | collective-permute-start | bytes 983048 | tf_op jit(solution)/shard_map/ppermute | solution.py:155
  14.8 1.4 collective-permute-start
  16.2 3.3 %collective-permute-start.4 = (bf16[2,320,256]{2,1,0:T(8,128)(2,1)}, bf16[2,320,256]{2,1,0:T(8,128)(2,1)}, u32[]{:S(2)}, u32[]{:S(2)}) collective-permute-start(bf16[2,320,256]{2,1,0:T(8,128)(2,1)} %get-tuple-element.59), channel_id=1, source_target_pairs={{0,128},{64,192},{128,0},{192,64},{1,129},{65,193},{129,1},{193,65... | collective-permute-start | bytes 983048 | tf_op jit(solution)/shard_map/ppermute | solution.py:159
  19.5 0.8 eq.81
  20.3 0.7 pad_add_fusion
  21.0 0.6 mark.2
  21.6 8.9 %all-to-all-start = ((s32[16,1,48]{2,1,0:T(1,128)}), s32[16,1,48]{2,1,0:T(1,128)S(1)}, u32[]{:S(2)}, u32[]{:S(2)}) async-start(s32[16,1,48]{2,1,0:T(1,128)} %bitcast.3), calls=%async_computation | async-start | bytes 16384 | tf_op jit(solution)/shard_map/all_to_all | solution.py:192
  30.5 0.8 constant_dynamic-slice_fusion
  31.3 1.0 copy.19
  32.3 1.1 maximum_maximum_fusion
  33.4 5.5 %all-to-all-done = s32[16,1,48]{2,1,0:T(1,128)S(1)} async-done(((s32[16,1,48]{2,1,0:T(1,128)}), s32[16,1,48]{2,1,0:T(1,128)S(1)}, u32[]{:S(2)}, u32[]{:S(2)}) %all-to-all-start) | async-done | bytes 3104 | tf_op jit(solution)/shard_map/all_to_all | solution.py:192
  38.9 4.3 %all-to-all-start.2 = ((bf16[16,48,640]{2,1,0:T(8,128)(2,1)}), bf16[16,48,640]{2,1,0:T(8,128)(2,1)}, u32[]{:S(2)}, u32[]{:S(2)}) async-start(bf16[16,48,640]{2,1,0:T(8,128)(2,1)} %maximum_maximum_fusion), calls=%async_computation.2 | async-start | bytes 1966080 | tf_op jit(solution)/shard_map/all_to_all | solution.py:193
  43.2 0.0 all-gather.3.cloned.1.call-start
  43.3 1.8 %collective-permute-start.8 = (bf16[2,320,256]{2,1,0:T(8,128)(2,1)}, bf16[2,320,256]{2,1,0:T(8,128)(2,1)S(1)}, u32[]{:S(2)}, u32[]{:S(2)}) collective-permute-start(bf16[2,320,256]{2,1,0:T(8,128)(2,1)} %collective-permute-done.3.refs_4_), channel_id=1, source_target_pairs={{0,16},{16,32},{32,48},{48,0},{1,17},{17,33},{33,49},{49,1},{2,18}... | collective-permute-start | bytes 983048 | tf_op jit(solution)/shard_map/ppermute | solution.py:155
  45.2 2.7 %collective-permute-start.7 = (bf16[2,320,256]{2,1,0:T(8,128)(2,1)}, bf16[2,320,256]{2,1,0:T(8,128)(2,1)S(1)}, u32[]{:S(2)}, u32[]{:S(2)}) collective-permute-start(bf16[2,320,256]{2,1,0:T(8,128)(2,1)} %collective-permute-done.3.refs_4_), channel_id=1, source_target_pairs={{0,32},{16,48},{32,0},{48,16},{1,33},{17,49},{33,1},{49,17},{2,34}... | collective-permute-start | bytes 983048 | tf_op jit(solution)/shard_map/ppermute | solution.py:155
  47.8 1.5 collective-permute-start.6
  49.3 1.5 collective-permute-start.5
  50.8 0.5 compare_select_fusion.4
  51.3 0.6 collective-permute-start.15
  51.9 16.7 %collective-permute-done.8.refs_7_ = bf16[2,320,256]{2,1,0:T(8,128)(2,1)S(1)} collective-permute-done((bf16[2,320,256]{2,1,0:T(8,128)(2,1)}, bf16[2,320,256]{2,1,0:T(8,128)(2,1)S(1)}, u32[]{:S(2)}, u32[]{:S(2)}) %collective-permute-start.8) | collective-permute-done | bytes 327712 | tf_op jit(solution)/shard_map/ppermute | solution.py:155
  68.6 4.3 %collective-permute-done.7.refs_6_ = bf16[2,320,256]{2,1,0:T(8,128)(2,1)S(1)} collective-permute-done((bf16[2,320,256]{2,1,0:T(8,128)(2,1)}, bf16[2,320,256]{2,1,0:T(8,128)(2,1)S(1)}, u32[]{:S(2)}, u32[]{:S(2)}) %collective-permute-start.7) | collective-permute-done | bytes 327712 | tf_op jit(solution)/shard_map/ppermute | solution.py:155
  72.9 0.7 copy-done.3
  73.6 0.1 copy-done.4
  73.7 0.7 copy-done.5
  74.5 2.2 %slice.30 = bf16[16,40,640]{2,1,0:T(8,128)(2,1)} slice(bf16[16,48,640]{2,1,0:T(8,128)(2,1)} %all-to-all-done.2), slice={[0:16], [0:40], [0:640]} | slice | bytes 1638400 | tf_op jit(solution)/shard_map/slice | solution.py:195
  76.7 0.0 all-gather.3.cloned.1.call-update
  76.7 0.3 convert_reduce_fusion
  77.1 0.1 select_reduce_fusion.1
  77.2 0.1 copy.15
  77.3 0.1 reshape.128.ids
  77.4 2.5 %copy-done.1 = bf16[16,32,5120]{2,1,0:T(8,128)(2,1)S(1)} copy-done((bf16[16,32,5120]{2,1,0:T(8,128)(2,1)S(1)}, bf16[16,32,5120]{2,1,0:T(8,128)(2,1)}, u32[]{:S(2)}) %copy-start.1) | copy-done | bytes 5242904
  79.9 1.4 pick_queries.1
  81.3 1.2 constant_dynamic-slice_fusion.1
  82.5 0.7 collective-permute-start.9
  83.2 5.5 %all-to-all-start.1 = ((bf16[8,2,32,640]{3,2,1,0:T(8,128)(2,1)}), bf16[8,2,32,640]{3,2,1,0:T(8,128)(2,1)}, u32[]{:S(2)}, u32[]{:S(2)}) async-start(bf16[8,2,32,640]{3,2,1,0:T(8,128)(2,1)} %bitcast.46), calls=%async_computation.1 | async-start | bytes 1310720 | tf_op jit(solution)/shard_map/all_to_all | solution.py:220
  88.7 0.6 collective-permute-start.13
  89.3 1.5 collective-permute-start.12
  90.8 1.6 collective-permute-start.11
  92.4 1.1 collective-permute-start.10
  93.4 0.2 convert_reduce_fusion.1
  93.6 6.0 %collective-permute-done.13.refs_9_ = bf16[2,320,256]{2,1,0:T(8,128)(2,1)} collective-permute-done((bf16[2,320,256]{2,1,0:T(8,128)(2,1)}, bf16[2,320,256]{2,1,0:T(8,128)(2,1)}, u32[]{:S(2)}, u32[]{:S(2)}) %collective-permute-start.13) | collective-permute-done | bytes 327712 | tf_op jit(solution)/shard_map/ppermute | solution.py:155
  99.6 7.7 %collective-permute-done.12.refs_15_ = bf16[2,320,256]{2,1,0:T(8,128)(2,1)} collective-permute-done((bf16[2,320,256]{2,1,0:T(8,128)(2,1)}, bf16[2,320,256]{2,1,0:T(8,128)(2,1)}, u32[]{:S(2)}, u32[]{:S(2)}) %collective-permute-start.12) | collective-permute-done | bytes 327712 | tf_op jit(solution)/shard_map/ppermute | solution.py:155
  107.3 5.6 %collective-permute-done.10.refs_13_ = bf16[2,320,256]{2,1,0:T(8,128)(2,1)} collective-permute-done((bf16[2,320,256]{2,1,0:T(8,128)(2,1)}, bf16[2,320,256]{2,1,0:T(8,128)(2,1)}, u32[]{:S(2)}, u32[]{:S(2)}) %collective-permute-start.10) | collective-permute-done | bytes 327712 | tf_op jit(solution)/shard_map/ppermute | solution.py:155
  112.9 5.4 %all-to-all-start.3 = ((bf16[8,2,32,640]{3,2,1,0:T(8,128)(2,1)}), bf16[8,2,32,640]{3,2,1,0:T(8,128)(2,1)}, u32[]{:S(2)}, u32[]{:S(2)}) async-start(bf16[8,2,32,640]{3,2,1,0:T(8,128)(2,1)} %bitcast.28), calls=%async_computation.3 | async-start | bytes 1310720 | tf_op jit(solution)/shard_map/all_to_all | solution.py:223
  118.4 0.1 stack.67.order
  118.5 0.1 broadcast_select_fusion.slot
  118.6 0.1 slice.32
  118.7 0.1 broadcast_in_dim.45
  118.7 0.2 select_reduce_fusion
  118.9 0.1 broadcast_select_fusion.1
  119.0 0.9 slice.31.refs_17_
  119.9 10.4 %all-to-all-done.3 = bf16[8,2,32,640]{3,2,1,0:T(8,128)(2,1)} async-done(((bf16[8,2,32,640]{3,2,1,0:T(8,128)(2,1)}), bf16[8,2,32,640]{3,2,1,0:T(8,128)(2,1)}, u32[]{:S(2)}, u32[]{:S(2)}) %all-to-all-start.3) | async-done | bytes 655392 | tf_op jit(solution)/shard_map/all_to_all | solution.py:223
  130.3 12.6 %attend.1 = f32[2,256]{1,0:T(2,128)S(1)} custom-call(s32[16]{0:T(128)S(1)} %stack.67.order, s32[16]{0:T(128)S(1)} %broadcast_select_fusion.slot, bf16[2,320,256]{2,1,0:T(8,128)(2,1)} %get-tuple-element.35.refs_0_, bf16[2,320,256]{2,1,0:T(8,128)(2,1)} %collective-permute-done.refs_1_, bf16[2,320,256]{2,1,0:T(8,128)(2,1)} %collective-permute-done.1.refs_2_, ...), custom_call_target="tpu_custom_call" | custom-call | flops 3355443200 | bytes 13631488 | tf_op jit(solution)/shard_map/attend/pallas_call | solution.py:114
  143.0 0.1 reshape.136
  143.0 0.2 select_reduce_fusion.2
  143.2 0.6 broadcast_in_dim.77
  143.8 7.3 %all-to-all-start.4 = ((f32[16,1,16]{2,1,0:T(1,128)}), f32[16,1,16]{2,1,0:T(1,128)S(1)}, u32[]{:S(2)}, u32[]{:S(2)}) async-start(f32[16,1,16]{2,1,0:T(1,128)} %broadcast_in_dim.77), calls=%async_computation.4 | async-start | bytes 16384 | tf_op jit(solution)/shard_map/all_to_all | solution.py:242
  151.2 0.1 convert_element_type.17
  151.2 7.8 %all-to-all-done.4 = f32[16,1,16]{2,1,0:T(1,128)S(1)} async-done(((f32[16,1,16]{2,1,0:T(1,128)}), f32[16,1,16]{2,1,0:T(1,128)S(1)}, u32[]{:S(2)}, u32[]{:S(2)}) %all-to-all-start.4) | async-done | bytes 1056 | tf_op jit(solution)/shard_map/all_to_all | solution.py:242
  159.1 0.1 reshape.138
  159.2 0.6 divide_select_fusion
  (43 shorter events, 0.2 us)
Async XLA Ops:
  6.5 23.9 %copy-start = (bf16[320,5120]{1,0:T(8,128)(2,1)S(1)}, bf16[320,5120]{1,0:T(8,128)(2,1)}, u32[]{:S(2)}) copy-start(bf16[320,5120]{1,0:T(8,128)(2,1)} %param.8) | copy-start | bytes 9830404
  8.6 34.7 %collective-permute-start.3 = (bf16[2,320,256]{2,1,0:T(8,128)(2,1)}, bf16[2,320,256]{2,1,0:T(8,128)(2,1)}, u32[]{:S(2)}, u32[]{:S(2)}) collective-permute-start(bf16[2,320,256]{2,1,0:T(8,128)(2,1)} %get-tuple-element.35.refs_0_), channel_id=1, source_target_pairs={{0,64},{64,0},{128,192},{192,128},{1,65},{65,1},{129,193},{193,129... | collective-permute-start | bytes 983048 | tf_op jit(solution)/shard_map/ppermute | solution.py:159
  10.6 32.7 %collective-permute-start.2 = (bf16[2,320,256]{2,1,0:T(8,128)(2,1)}, bf16[2,320,256]{2,1,0:T(8,128)(2,1)}, u32[]{:S(2)}, u32[]{:S(2)}) collective-permute-start(bf16[2,320,256]{2,1,0:T(8,128)(2,1)} %get-tuple-element.35.refs_0_), channel_id=1, source_target_pairs={{0,16},{16,32},{32,48},{48,0},{1,17},{17,33},{33,49},{49,1},{2,18}... | collective-permute-start | bytes 983048 | tf_op jit(solution)/shard_map/ppermute | solution.py:155
  12.1 31.3 %collective-permute-start.1 = (bf16[2,320,256]{2,1,0:T(8,128)(2,1)}, bf16[2,320,256]{2,1,0:T(8,128)(2,1)}, u32[]{:S(2)}, u32[]{:S(2)}) collective-permute-start(bf16[2,320,256]{2,1,0:T(8,128)(2,1)} %get-tuple-element.35.refs_0_), channel_id=1, source_target_pairs={{0,32},{16,48},{32,0},{48,16},{1,33},{17,49},{33,1},{49,17},{2,34}... | collective-permute-start | bytes 983048 | tf_op jit(solution)/shard_map/ppermute | solution.py:155
  14.8 28.5 %collective-permute-start = (bf16[2,320,256]{2,1,0:T(8,128)(2,1)}, bf16[2,320,256]{2,1,0:T(8,128)(2,1)}, u32[]{:S(2)}, u32[]{:S(2)}) collective-permute-start(bf16[2,320,256]{2,1,0:T(8,128)(2,1)} %get-tuple-element.35.refs_0_), channel_id=1, source_target_pairs={{0,48},{16,0},{32,16},{48,32},{1,49},{17,1},{33,17},{49,33},{2,50}... | collective-permute-start | bytes 983048 | tf_op jit(solution)/shard_map/ppermute | solution.py:155
  16.2 27.1 %collective-permute-start.4 = (bf16[2,320,256]{2,1,0:T(8,128)(2,1)}, bf16[2,320,256]{2,1,0:T(8,128)(2,1)}, u32[]{:S(2)}, u32[]{:S(2)}) collective-permute-start(bf16[2,320,256]{2,1,0:T(8,128)(2,1)} %get-tuple-element.59), channel_id=1, source_target_pairs={{0,128},{64,192},{128,0},{192,64},{1,129},{65,193},{129,1},{193,65... | collective-permute-start | bytes 983048 | tf_op jit(solution)/shard_map/ppermute | solution.py:159
  20.3 30.6 %copy-start.7 = (s32[32]{0:T(128)}, s32[32]{0:T(128)S(1)}, u32[]{:S(2)}) copy-start(s32[32]{0:T(128)S(1)} %eq.81) | copy-start | bytes 388
  21.0 10.3 %copy-start.6 = (bf16[320,40]{0,1:T(8,128)(2,1)S(1)}, bf16[320,40]{0,1:T(8,128)(2,1)}, u32[]{:S(2)}) copy-start(bf16[320,40]{0,1:T(8,128)(2,1)} %param.9) | copy-start | bytes 76804
  21.6 17.3 %all-to-all-start = ((s32[16,1,48]{2,1,0:T(1,128)}), s32[16,1,48]{2,1,0:T(1,128)S(1)}, u32[]{:S(2)}, u32[]{:S(2)}) async-start(s32[16,1,48]{2,1,0:T(1,128)} %bitcast.3), calls=%async_computation | async-start | bytes 16384 | tf_op jit(solution)/shard_map/all_to_all | solution.py:192
  38.9 35.6 %all-to-all-start.2 = ((bf16[16,48,640]{2,1,0:T(8,128)(2,1)}), bf16[16,48,640]{2,1,0:T(8,128)(2,1)}, u32[]{:S(2)}, u32[]{:S(2)}) async-start(bf16[16,48,640]{2,1,0:T(8,128)(2,1)} %maximum_maximum_fusion), calls=%async_computation.2 | async-start | bytes 1966080 | tf_op jit(solution)/shard_map/all_to_all | solution.py:193
  43.2 87.1 %all-gather.3.cloned.1.call-start = ((), (), s32[]{:S(2)}) async-start(), calls=%async_computation.5 | async-start | bytes 7372800 | tf_op jit(solution)/shard_map/all_gather | solution.py:195
  43.3 25.3 %collective-permute-start.8 = (bf16[2,320,256]{2,1,0:T(8,128)(2,1)}, bf16[2,320,256]{2,1,0:T(8,128)(2,1)S(1)}, u32[]{:S(2)}, u32[]{:S(2)}) collective-permute-start(bf16[2,320,256]{2,1,0:T(8,128)(2,1)} %collective-permute-done.3.refs_4_), channel_id=1, source_target_pairs={{0,16},{16,32},{32,48},{48,0},{1,17},{17,33},{33,49},{49,1},{2,18}... | collective-permute-start | bytes 983048 | tf_op jit(solution)/shard_map/ppermute | solution.py:155
  45.2 27.7 %collective-permute-start.7 = (bf16[2,320,256]{2,1,0:T(8,128)(2,1)}, bf16[2,320,256]{2,1,0:T(8,128)(2,1)S(1)}, u32[]{:S(2)}, u32[]{:S(2)}) collective-permute-start(bf16[2,320,256]{2,1,0:T(8,128)(2,1)} %collective-permute-done.3.refs_4_), channel_id=1, source_target_pairs={{0,32},{16,48},{32,0},{48,16},{1,33},{17,49},{33,1},{49,17},{2,34}... | collective-permute-start | bytes 983048 | tf_op jit(solution)/shard_map/ppermute | solution.py:155
  47.8 25.0 %collective-permute-start.6 = (bf16[2,320,256]{2,1,0:T(8,128)(2,1)}, bf16[2,320,256]{2,1,0:T(8,128)(2,1)S(1)}, u32[]{:S(2)}, u32[]{:S(2)}) collective-permute-start(bf16[2,320,256]{2,1,0:T(8,128)(2,1)} %collective-permute-done.3.refs_4_), channel_id=1, source_target_pairs={{0,48},{16,0},{32,16},{48,32},{1,49},{17,1},{33,17},{49,33},{2,50}... | collective-permute-start | bytes 983048 | tf_op jit(solution)/shard_map/ppermute | solution.py:155
  49.3 23.6 %collective-permute-start.5 = (bf16[2,320,256]{2,1,0:T(8,128)(2,1)}, bf16[2,320,256]{2,1,0:T(8,128)(2,1)S(1)}, u32[]{:S(2)}, u32[]{:S(2)}) collective-permute-start(bf16[2,320,256]{2,1,0:T(8,128)(2,1)} %collective-permute-done.4.refs_8_), channel_id=1, source_target_pairs={{0,64},{64,0},{128,192},{192,128},{1,65},{65,1},{129,193},{193,129... | collective-permute-start | bytes 983048 | tf_op jit(solution)/shard_map/ppermute | solution.py:159
  51.3 39.4 %collective-permute-start.15 = (bf16[2,320,256]{2,1,0:T(8,128)(2,1)}, bf16[2,320,256]{2,1,0:T(8,128)(2,1)}, u32[]{:S(2)}, u32[]{:S(2)}) collective-permute-start(bf16[2,320,256]{2,1,0:T(8,128)(2,1)} %collective-permute-done.4.refs_8_), channel_id=1, source_target_pairs={{0,16},{16,32},{32,48},{48,0},{1,17},{17,33},{33,49},{49,1},{2,18}... | collective-permute-start | bytes 983048 | tf_op jit(solution)/shard_map/ppermute | solution.py:155
  68.6 4.3 %copy-start.2 = (bf16[2,320,256]{2,1,0:T(8,128)(2,1)}, bf16[2,320,256]{2,1,0:T(8,128)(2,1)S(1)}, u32[]{:S(2)}) copy-start(bf16[2,320,256]{2,1,0:T(8,128)(2,1)S(1)} %collective-permute-done.8.refs_7_) | copy-start | bytes 983044
  68.6 23.8 %collective-permute-start.14 = (bf16[2,320,256]{2,1,0:T(8,128)(2,1)}, bf16[2,320,256]{2,1,0:T(8,128)(2,1)}, u32[]{:S(2)}, u32[]{:S(2)}) collective-permute-start(bf16[2,320,256]{2,1,0:T(8,128)(2,1)} %collective-permute-done.4.refs_8_), channel_id=1, source_target_pairs={{0,32},{16,48},{32,0},{48,16},{1,33},{17,49},{33,1},{49,17},{2,34}... | collective-permute-start | bytes 983048 | tf_op jit(solution)/shard_map/ppermute | solution.py:155
  72.9 0.7 copy-start.3
  72.9 0.8 copy-start.4
  73.7 0.7 copy-start.5
  77.4 2.5 %copy-start.1 = (bf16[16,32,5120]{2,1,0:T(8,128)(2,1)S(1)}, bf16[16,32,5120]{2,1,0:T(8,128)(2,1)}, u32[]{:S(2)}) copy-start(bf16[16,32,5120]{2,1,0:T(8,128)(2,1)} %q_ref.1) | copy-start | bytes 15728644
  81.3 12.1 %copy-start.9 = (s32[32]{0:T(128)S(1)}, s32[32]{0:T(128)}, u32[]{:S(2)}) copy-start(s32[32]{0:T(128)} %get-tuple-element.62) | copy-start | bytes 388
  82.5 36.2 %copy-start.8 = (s32[32]{0:T(128)S(1)}, s32[32]{0:T(128)}, u32[]{:S(2)}) copy-start(s32[32]{0:T(128)} %copy-done.7) | copy-start | bytes 388
  82.5 30.4 %collective-permute-start.9 = (bf16[4,2,2,32,640]{4,3,2,1,0:T(8,128)(2,1)}, bf16[4,2,2,32,640]{4,3,2,1,0:T(8,128)(2,1)}, u32[]{:S(2)}, u32[]{:S(2)}) collective-permute-start(bf16[4,2,2,32,640]{4,3,2,1,0:T(8,128)(2,1)} %get-tuple-element.58), channel_id=1, source_target_pairs={{0,194},{2,192},{64,130},{66,128},{128,66},{130,64},{192,2},{194,0... | collective-permute-start | bytes 1966088 | tf_op jit(solution)/shard_map/ppermute | solution.py:219
  83.2 29.7 %all-to-all-start.1 = ((bf16[8,2,32,640]{3,2,1,0:T(8,128)(2,1)}), bf16[8,2,32,640]{3,2,1,0:T(8,128)(2,1)}, u32[]{:S(2)}, u32[]{:S(2)}) async-start(bf16[8,2,32,640]{3,2,1,0:T(8,128)(2,1)} %bitcast.46), calls=%async_computation.1 | async-start | bytes 1310720 | tf_op jit(solution)/shard_map/all_to_all | solution.py:220
  88.7 10.9 %collective-permute-start.13 = (bf16[2,320,256]{2,1,0:T(8,128)(2,1)}, bf16[2,320,256]{2,1,0:T(8,128)(2,1)}, u32[]{:S(2)}, u32[]{:S(2)}) collective-permute-start(bf16[2,320,256]{2,1,0:T(8,128)(2,1)} %collective-permute-done.4.refs_8_), channel_id=1, source_target_pairs={{0,48},{16,0},{32,16},{48,32},{1,49},{17,1},{33,17},{49,33},{2,50}... | collective-permute-start | bytes 983048 | tf_op jit(solution)/shard_map/ppermute | solution.py:155
  89.3 18.0 %collective-permute-start.12 = (bf16[2,320,256]{2,1,0:T(8,128)(2,1)}, bf16[2,320,256]{2,1,0:T(8,128)(2,1)}, u32[]{:S(2)}, u32[]{:S(2)}) collective-permute-start(bf16[2,320,256]{2,1,0:T(8,128)(2,1)} %copy-done.5), channel_id=1, source_target_pairs={{0,16},{16,32},{32,48},{48,0},{1,17},{17,33},{33,49},{49,1},{2,18}... | collective-permute-start | bytes 983048 | tf_op jit(solution)/shard_map/ppermute | solution.py:155
  90.8 16.6 %collective-permute-start.11 = (bf16[2,320,256]{2,1,0:T(8,128)(2,1)}, bf16[2,320,256]{2,1,0:T(8,128)(2,1)}, u32[]{:S(2)}, u32[]{:S(2)}) collective-permute-start(bf16[2,320,256]{2,1,0:T(8,128)(2,1)} %copy-done.5), channel_id=1, source_target_pairs={{0,32},{16,48},{32,0},{48,16},{1,33},{17,49},{33,1},{49,17},{2,34}... | collective-permute-start | bytes 983048 | tf_op jit(solution)/shard_map/ppermute | solution.py:155
  92.4 20.5 %collective-permute-start.10 = (bf16[2,320,256]{2,1,0:T(8,128)(2,1)}, bf16[2,320,256]{2,1,0:T(8,128)(2,1)}, u32[]{:S(2)}, u32[]{:S(2)}) collective-permute-start(bf16[2,320,256]{2,1,0:T(8,128)(2,1)} %copy-done.5), channel_id=1, source_target_pairs={{0,48},{16,0},{32,16},{48,32},{1,49},{17,1},{33,17},{49,33},{2,50}... | collective-permute-start | bytes 983048 | tf_op jit(solution)/shard_map/ppermute | solution.py:155
  112.9 17.4 %all-to-all-start.3 = ((bf16[8,2,32,640]{3,2,1,0:T(8,128)(2,1)}), bf16[8,2,32,640]{3,2,1,0:T(8,128)(2,1)}, u32[]{:S(2)}, u32[]{:S(2)}) async-start(bf16[8,2,32,640]{3,2,1,0:T(8,128)(2,1)} %bitcast.28), calls=%async_computation.3 | async-start | bytes 1310720 | tf_op jit(solution)/shard_map/all_to_all | solution.py:223
  130.3 28.9 %copy-start.10 = (s32[4]{0:T(128)S(1)}, s32[4]{0:T(128)}, u32[]{:S(2)}) copy-start(s32[4]{0:T(128)} %param.13) | copy-start | bytes 52
  143.8 15.2 %all-to-all-start.4 = ((f32[16,1,16]{2,1,0:T(1,128)}), f32[16,1,16]{2,1,0:T(1,128)S(1)}, u32[]{:S(2)}, u32[]{:S(2)}) async-start(f32[16,1,16]{2,1,0:T(1,128)} %broadcast_in_dim.77), calls=%async_computation.4 | async-start | bytes 16384 | tf_op jit(solution)/shard_map/all_to_all | solution.py:242
Sparse Core Ops, SparseCore 0:
  76.8 49.8 all-gather.2

commit v3 on v2

--- a/solution.py
+++ b/solution.py
@@ -19,6 +19,7 @@
 GW = GH * HD
 PATCH = 256
 FEAT = 320
+ROWS = FEAT // 8
 TP = ("zl", "x")
 DP = ("y", "zh", "c")
 YC = ("y", "c")
@@ -54,10 +55,10 @@
     )(ids, col, queries)
 
 
-def attend_kernel(order, slot, *refs):
+def keys_kernel(order, *refs):
     units = refs[:16]
-    w_ref, v_ref, near_ref, far_ref, o_ref = refs[16:21]
-    ws, q_ref, acc, val, wsem = refs[21:]
+    w_ref, v_ref, acc, val = refs[16:20]
+    ws, wsem = refs[20:]
     wcopy = [pltpu.make_async_copy(w_ref.at[:, order[u]], ws.at[u], wsem.at[u]) for u in range(16)]
     for u in range(16):
         wcopy[u].start()
@@ -82,6 +83,33 @@
             else:
                 acc[i] += keys
                 val[i] += values
+
+
+def project(order, units, w, v):
+    vmem = pl.BlockSpec(memory_space=pltpu.VMEM)
+    return pl.pallas_call(
+        keys_kernel,
+        out_shape=(
+            jax.ShapeDtypeStruct((2, PATCH, GW), jnp.float32),
+            jax.ShapeDtypeStruct((2, 8, PATCH), jnp.float32),
+        ),
+        in_specs=[pl.BlockSpec(memory_space=pltpu.SMEM)]
+        + [vmem] * 16
+        + [pl.BlockSpec(memory_space=pltpu.HBM), vmem],
+        out_specs=(vmem, vmem),
+        scratch_shapes=[
+            pltpu.VMEM((16, 8, ROWS, GW), jnp.bfloat16),
+            pltpu.SemaphoreType.DMA((16,)),
+        ],
+        compiler_params=pltpu.CompilerParams(vmem_limit_bytes=44 * 2**20),
+        cost_estimate=pl.CostEstimate(
+            flops=2 * 512 * 5120 * 640, bytes_accessed=13 * 2**20, transcendentals=0
+        ),
+        name="project",
+    )(order, *units, w, v)
+
+
+def attend_kernel(slot, acc, val, near_ref, far_ref, o_ref, q_ref):
     q_ref[0:CAP_DP] = near_ref[...]
     q_ref[CAP_DP:] = far_ref[...]
     scale = float(HD) ** (-0.5)
@@ -109,28 +137,20 @@
         o_ref[i : i + 1, :] = total
 
 
-def attend(order, slot, units, w, v, near, far):
+def attend(slot, keys, values, near, far):
     vmem = pl.BlockSpec(memory_space=pltpu.VMEM)
     return pl.pallas_call(
         attend_kernel,
         out_shape=jax.ShapeDtypeStruct((2, TOP * L), jnp.float32),
-        in_specs=[pl.BlockSpec(memory_space=pltpu.SMEM)] * 2
-        + [vmem] * 16
-        + [pl.BlockSpec(memory_space=pltpu.HBM)] + [vmem] * 3,
+        in_specs=[pl.BlockSpec(memory_space=pltpu.SMEM)] + [vmem] * 4,
         out_specs=vmem,
-        scratch_shapes=[
-            pltpu.VMEM((16, GROUPS, FEAT // 8, GW), jnp.bfloat16),
-            pltpu.VMEM((2 * CAP_DP, L, GW), jnp.bfloat16),
-            pltpu.VMEM((2, PATCH, GW), jnp.float32),
-            pltpu.VMEM((2, 8, PATCH), jnp.float32),
-            pltpu.SemaphoreType.DMA((16,)),
-        ],
-        compiler_params=pltpu.CompilerParams(vmem_limit_bytes=52 * 2**20),
+        scratch_shapes=[pltpu.VMEM((2 * CAP_DP, L, GW), jnp.bfloat16)],
+        compiler_params=pltpu.CompilerParams(vmem_limit_bytes=40 * 2**20),
         cost_estimate=pl.CostEstimate(
-            flops=2 * 512 * 5120 * 640, bytes_accessed=13 * 2**20, transcendentals=655360
+            flops=2 * 3 * 10 * 256 * 256 * 128, bytes_accessed=4 * 2**20, transcendentals=655360
         ),
         name="attend",
-    )(order, slot, *units, w, v, near, far)
+    )(slot, keys, values, near, far)
 
 
 def mark_kernel(x_ref, o_ref):
@@ -138,7 +158,8 @@
 
 
 def mark(token, *held):
-    token, *held = lax.optimization_barrier((token, *held))
+    if held:
+        token, *held = lax.optimization_barrier((token, *held))
     token = pl.pallas_call(
         mark_kernel,
         out_shape=jax.ShapeDtypeStruct(token.shape, token.dtype),
@@ -170,9 +191,8 @@
     me = lax.axis_index(DP)
     part = lax.axis_index(YC)
 
-    rows = FEAT // 8
-    w_part = lax.dynamic_slice_in_dim(key_weight, part * rows, rows, axis=0)
-    w_part = jnp.swapaxes(w_part.reshape(rows, GROUPS, GW), 0, 1)
+    w_part = lax.dynamic_slice_in_dim(key_weight, part * ROWS, ROWS, axis=0)
+    w_part = jnp.swapaxes(w_part.reshape(ROWS, GROUPS, GW), 0, 1)
     v_part = jnp.pad(value_map.T.reshape(GROUPS, GH, FEAT), ((0, 0), (0, 8 - GH), (0, GW - FEAT)))
     w_part = jnp.concatenate([w_part, v_part], axis=1)
     w_sent = jnp.concatenate([w_part, w_part], axis=0)
@@ -188,17 +208,20 @@
     slot_total = IMG * TOP
     cand_ids = candidates.reshape(slot_total)
     notice = jnp.broadcast_to(jnp.concatenate([cand_ids, cap_lengths])[None], (16, slot_total + CAP_DP))
-    notice, mine, theirs = mark(notice, mine, theirs)
+    notice, w_sent = mark(notice, w_sent)
+    w_sent, notice = lax.optimization_barrier((w_sent, notice))
+    w_mine = lax.all_to_all(w_sent, TP, split_axis=0, concat_axis=0, tiled=True)
+    w_mine, v_all = w_mine[:, :ROWS], w_mine[:, ROWS:, :FEAT]
+    w_mine, v_all, notice, own, beside, over = lax.optimization_barrier(
+        (w_mine, v_all, notice, own, beside, over)
+    )
+    w_all = lax.all_gather(w_mine, YC)
+    last = flip(over, 1)
+    beside = ring(beside)
+    (notice,) = mark(notice)
     notices = lax.all_to_all(notice, DP, split_axis=0, concat_axis=0, tiled=True)
-    w_mine = lax.all_to_all(w_sent, TP, split_axis=0, concat_axis=0, tiled=True)
-    w_mine, img_tokens = lax.optimization_barrier((w_mine, img_tokens))
-    w_all = lax.all_gather(w_mine[:, :rows], YC)
-    v_all = w_mine[:, rows:, :FEAT]
-
-    notices, own, beside, over = lax.optimization_barrier((notices, own, beside, over))
-    last = flip(over, 1)
-    beside, over = ring(beside), ring(over)
-    notices, last, *beside = mark(notices, last, *beside)
+    notices, beside, last = lax.optimization_barrier((notices, beside, last))
+    over = ring(over)
 
     asked = notices[:, :slot_total]
     lengths = notices[:, slot_total:].reshape(16 * CAP_DP)
@@ -234,7 +257,8 @@
         jnp.where(cand_ids[:, None] == jnp.arange(16 * CAP_DP, dtype=jnp.int32)[None, :], lengths[None, :], 0), axis=1
     )
 
-    attended = attend(order, slot, units, w_all, v_all, near, far)
+    keys, values = project(order, units, w_all, v_all)
+    attended = attend(slot, keys, values, near, far)
 
     my_lengths = jnp.where(half == 0, slot_lengths[:16], slot_lengths[16:])
     live = jnp.arange(L, dtype=jnp.int32)[None, :] < my_lengths[:, None]

time: 167 us -> 162 us (0.970)
  waiting for transfers between devices: 64 us -> 58.4 us
    ppermute x12, waiting for transfers between devices: 40.3 us -> 18.4 us  [shift(): return lax.ppermute(block, axis, [(i, (i + by) % 4) for i in range(4)])]
    all_to_all x1, waiting for transfers between devices: 0.01 us -> 18.2 us  [local(): w_mine = lax.all_to_all(w_sent, TP, split_axis=0, concat_axis=0, tiled=True)]
    pallas_call x0 -> x1, Pallas kernels: none -> 10.6 us  [project(): pl.pallas_call(keys_kernel, out_shape=(jax.ShapeDtypeStruct((2, PATCH, GW...]
    all_to_all x1, waiting for transfers between devices: 10.4 us -> 0.01 us  [local(): lax.all_to_all(far.reshape(8, 2, L, GW), YC, split_axis=0, concat_axis=0,...]
    pallas_call x1, Pallas kernels: 12.6 us -> 3.3 us  [attend(): pl.pallas_call(attend_kernel, out_shape=jax.ShapeDtypeStruct((2, TOP * L)...]
    ppermute x3, waiting for transfers between devices: 0.01 us -> 4.8 us  [flip(): return lax.ppermute(block, 'zl', [(i, i ^ mask) for i in range(4)])]
    all_to_all x1, starting transfers between devices: 4.33 us -> 8.51 us  [local(): w_mine = lax.all_to_all(w_sent, TP, split_axis=0, concat_axis=0, tiled=True)]
    all_to_all x1, starting transfers between devices: 7.32 us -> 3.42 us  [local(): lax.all_to_all(jnp.broadcast_to(sums[None], (16, 2 * TOP)), TP, split_axi...]
  transfers between devices with their start and end apart: 22 -> 22, of which waited for: 8 -> 8; matrix products, arithmetic and copies ran while one was open for 6% -> 5% of each run, Pallas kernels for 1% -> 8%
where the time goes in v3:
time: 162 us; the launch traced here: 161 us
  waiting for transfers between devices  58.4 us (36%)
  starting transfers between devices  54.3 us (34%)
  Pallas kernels  16 us (10%)
  local copies, waits for them, and re-layouts  14.4 us (9%)
  between operations  13.7 us (8%)
  other arithmetic  4.17 us (3%)
    ppermute x12, waiting for transfers between devices, shift(): return lax.ppermute(block, axis, [(i, (i + by) % 4) for i in range(4)])  18.4 us
    ppermute x12, starting transfers between devices, shift(): return lax.ppermute(block, axis, [(i, (i + by) % 4) for i in range(4)])  18.2 us
    all_to_all x1, waiting for transfers between devices, local(): w_mine = lax.all_to_all(w_sent, TP, split_axis=0, concat_axis=0, tiled=True)  18.2 us
    pallas_call x1, Pallas kernels, project(): pl.pallas_call(keys_kernel, out_shape=(jax.ShapeDtypeStruct((2, PATCH, GW...  10.6 us
    all_to_all x1, starting transfers between devices, local(): lax.all_to_all(notice, DP, split_axis=0, concat_axis=0, tiled=True)  8.86 us
    all_to_all x1, starting transfers between devices, local(): w_mine = lax.all_to_all(w_sent, TP, split_axis=0, concat_axis=0, tiled=True)  8.51 us
    all_to_all x1, waiting for transfers between devices, local(): lax.all_to_all(jnp.broadcast_to(sums[None], (16, 2 * TOP)), TP, split_axi...  7.77 us
    all_to_all x1, waiting for transfers between devices, local(): lax.all_to_all(notice, DP, split_axis=0, concat_axis=0, tiled=True)  7.03 us
  transfers between devices with their start and end apart: 22, of which 8 were waited for; matrix products, arithmetic and copies ran while one was open for 5% of the time, Pallas kernels for 8%

profile of v3, /device:TPU:8, one launch (start us, length us, event | category | flops | bytes accessed | tf_op | source)
XLA Modules:
  0.0 161.0 jit_solution(15458874901092927455)
XLA Ops:
  6.5 0.9 eq.81
  7.5 0.9 reshape.129
  8.3 0.2 copy-done
  8.6 0.7 pad_add_fusion
  9.3 1.0 maximum_maximum_fusion
  10.4 8.5 %all-to-all-start = ((bf16[16,48,640]{2,1,0:T(8,128)(2,1)}), bf16[16,48,640]{2,1,0:T(8,128)(2,1)}, u32[]{:S(2)}, u32[]{:S(2)}) async-start(bf16[16,48,640]{2,1,0:T(8,128)(2,1)} %maximum_maximum_fusion), calls=%async_computation | async-start | bytes 1966080 | tf_op jit(solution)/shard_map/all_to_all | solution.py:213
  18.9 0.0 all-gather.3.cloned.1.call-start
  18.9 2.0 %dynamic-slice_bitcast_fusion.1 = (bf16[2,320,256]{2,1,0:T(8,128)(2,1)}, bf16[2,320,256]{2,1,0:T(8,128)(2,1)}) fusion(bf16[256,4,320]{0,2,1:T(8,128)(2,1)} %param.7, s32[]{:T(128)S(6)} %select_n.153, s32[]{:T(128)S(6)} %select_n.152), kind=kLoop, calls=%fused_computation.3 | loop fusion | bytes 1310728 | tf_op jit(solution)/shard_map/dynamic_slice | solution.py:202
  20.9 2.8 %collective-permute-start.4 = (bf16[2,320,256]{2,1,0:T(8,128)(2,1)}, bf16[2,320,256]{2,1,0:T(8,128)(2,1)}, u32[]{:S(2)}, u32[]{:S(2)}) collective-permute-start(bf16[2,320,256]{2,1,0:T(8,128)(2,1)} %get-tuple-element.71), channel_id=1, source_target_pairs={{0,128},{64,192},{128,0},{192,64},{1,129},{65,193},{129,1},{193,65... | collective-permute-start | bytes 983048 | tf_op jit(solution)/shard_map/ppermute | solution.py:180
  23.7 1.5 collective-permute-start.3
  25.2 1.5 collective-permute-start.2
  26.6 2.7 %collective-permute-start.1 = (bf16[2,320,256]{2,1,0:T(8,128)(2,1)}, bf16[2,320,256]{2,1,0:T(8,128)(2,1)}, u32[]{:S(2)}, u32[]{:S(2)}) collective-permute-start(bf16[2,320,256]{2,1,0:T(8,128)(2,1)} %get-tuple-element.44.refs_0_), channel_id=1, source_target_pairs={{0,32},{16,48},{32,0},{48,16},{1,33},{17,49},{33,1},{49,17},{2,34}... | collective-permute-start | bytes 983048 | tf_op jit(solution)/shard_map/ppermute | solution.py:176
  29.3 1.5 collective-permute-start
  30.8 0.5 compare_select_fusion.4
  31.3 18.2 %all-to-all-done = bf16[16,48,640]{2,1,0:T(8,128)(2,1)} async-done(((bf16[16,48,640]{2,1,0:T(8,128)(2,1)}), bf16[16,48,640]{2,1,0:T(8,128)(2,1)}, u32[]{:S(2)}, u32[]{:S(2)}) %all-to-all-start) | async-done | bytes 983072 | tf_op jit(solution)/shard_map/all_to_all | solution.py:213
  49.4 0.9 slice.33.refs_17_
  50.3 2.1 %slice.32 = bf16[16,40,640]{2,1,0:T(8,128)(2,1)} slice(bf16[16,48,640]{2,1,0:T(8,128)(2,1)} %all-to-all-done), slice={[0:16], [0:40], [0:640]} | slice | bytes 1638400 | tf_op jit(solution)/shard_map/slice | solution.py:214
  52.5 4.8 %collective-permute-done.4.refs_8_ = bf16[2,320,256]{2,1,0:T(8,128)(2,1)} collective-permute-done((bf16[2,320,256]{2,1,0:T(8,128)(2,1)}, bf16[2,320,256]{2,1,0:T(8,128)(2,1)}, u32[]{:S(2)}, u32[]{:S(2)}) %collective-permute-start.4) | collective-permute-done | bytes 327712 | tf_op jit(solution)/shard_map/ppermute | solution.py:180
  57.3 1.5 collective-permute-start.7
  58.8 2.7 %collective-permute-start.6 = (bf16[2,320,256]{2,1,0:T(8,128)(2,1)}, bf16[2,320,256]{2,1,0:T(8,128)(2,1)}, u32[]{:S(2)}, u32[]{:S(2)}) collective-permute-start(bf16[2,320,256]{2,1,0:T(8,128)(2,1)} %collective-permute-done.3.refs_4_), channel_id=1, source_target_pairs={{0,32},{16,48},{32,0},{48,16},{1,33},{17,49},{33,1},{49,17},{2,34}... | collective-permute-start | bytes 983048 | tf_op jit(solution)/shard_map/ppermute | solution.py:176
  61.5 1.5 collective-permute-start.5
  62.9 0.0 all-gather.3.cloned.1.call-update
  63.0 0.1 collective-permute-start.8
  63.1 0.6 mark.3
  63.7 8.9 %all-to-all-start.1 = ((s32[16,1,48]{2,1,0:T(1,128)}), s32[16,1,48]{2,1,0:T(1,128)S(1)}, u32[]{:S(2)}, u32[]{:S(2)}) async-start(s32[16,1,48]{2,1,0:T(1,128)} %bitcast.5), calls=%async_computation.1 | async-start | bytes 16384 | tf_op jit(solution)/shard_map/all_to_all | solution.py:222
  72.6 0.6 collective-permute-start.15
  73.2 0.9 collective-permute-start.14
  74.1 7.0 %all-to-all-done.1 = s32[16,1,48]{2,1,0:T(1,128)S(1)} async-done(((s32[16,1,48]{2,1,0:T(1,128)}), s32[16,1,48]{2,1,0:T(1,128)S(1)}, u32[]{:S(2)}, u32[]{:S(2)}) %all-to-all-start.1) | async-done | bytes 3104 | tf_op jit(solution)/shard_map/all_to_all | solution.py:222
  81.2 0.3 convert_reduce_fusion
  81.5 0.1 select_reduce_fusion.1
  81.7 0.1 copy.16
  81.8 0.1 reshape.130.ids
  81.9 2.6 %copy-done.3 = bf16[16,32,5120]{2,1,0:T(8,128)(2,1)S(1)} copy-done((bf16[16,32,5120]{2,1,0:T(8,128)(2,1)S(1)}, bf16[16,32,5120]{2,1,0:T(8,128)(2,1)}, u32[]{:S(2)}) %copy-start.3) | copy-done | bytes 5242904
  84.4 1.4 pick_queries.1
  85.9 1.2 constant_dynamic-slice_fusion
  87.1 5.4 %all-to-all-start.2 = ((bf16[8,2,32,640]{3,2,1,0:T(8,128)(2,1)}), bf16[8,2,32,640]{3,2,1,0:T(8,128)(2,1)}, u32[]{:S(2)}, u32[]{:S(2)}) async-start(bf16[8,2,32,640]{3,2,1,0:T(8,128)(2,1)} %bitcast.44), calls=%async_computation.2 | async-start | bytes 1310720 | tf_op jit(solution)/shard_map/all_to_all | solution.py:243
  92.4 0.2 convert_reduce_fusion.1
  92.6 0.2 collective-permute-start.13
  92.8 1.9 %collective-permute-start.12 = (bf16[2,320,256]{2,1,0:T(8,128)(2,1)}, bf16[2,320,256]{2,1,0:T(8,128)(2,1)}, u32[]{:S(2)}, u32[]{:S(2)}) collective-permute-start(bf16[2,320,256]{2,1,0:T(8,128)(2,1)} %collective-permute-done.8.refs_12_), channel_id=1, source_target_pairs={{0,16},{16,32},{32,48},{48,0},{1,17},{17,33},{33,49},{49,1},{2,18}... | collective-permute-start | bytes 983048 | tf_op jit(solution)/shard_map/ppermute | solution.py:176
  94.7 0.7 collective-permute-start.11
  95.4 2.6 %collective-permute-start.10 = (bf16[2,320,256]{2,1,0:T(8,128)(2,1)}, bf16[2,320,256]{2,1,0:T(8,128)(2,1)}, u32[]{:S(2)}, u32[]{:S(2)}) collective-permute-start(bf16[2,320,256]{2,1,0:T(8,128)(2,1)} %collective-permute-done.8.refs_12_), channel_id=1, source_target_pairs={{0,48},{16,0},{32,16},{48,32},{1,49},{17,1},{33,17},{49,33},{2,50}... | collective-permute-start | bytes 983048 | tf_op jit(solution)/shard_map/ppermute | solution.py:176
  98.1 0.1 stack.67.order
  98.2 0.1 broadcast_select_fusion.slot
  98.3 0.1 slice.26
  98.4 0.1 broadcast_in_dim.45
  98.4 5.1 %collective-permute-done.13.refs_9_ = bf16[2,320,256]{2,1,0:T(8,128)(2,1)} collective-permute-done((bf16[2,320,256]{2,1,0:T(8,128)(2,1)}, bf16[2,320,256]{2,1,0:T(8,128)(2,1)}, u32[]{:S(2)}, u32[]{:S(2)}) %collective-permute-start.13) | collective-permute-done | bytes 327712 | tf_op jit(solution)/shard_map/ppermute | solution.py:176
  103.6 7.5 %collective-permute-done.12.refs_15_ = bf16[2,320,256]{2,1,0:T(8,128)(2,1)} collective-permute-done((bf16[2,320,256]{2,1,0:T(8,128)(2,1)}, bf16[2,320,256]{2,1,0:T(8,128)(2,1)}, u32[]{:S(2)}, u32[]{:S(2)}) %collective-permute-start.12) | collective-permute-done | bytes 327712 | tf_op jit(solution)/shard_map/ppermute | solution.py:176
  111.1 5.8 %collective-permute-done.10.refs_13_ = bf16[2,320,256]{2,1,0:T(8,128)(2,1)} collective-permute-done((bf16[2,320,256]{2,1,0:T(8,128)(2,1)}, bf16[2,320,256]{2,1,0:T(8,128)(2,1)}, u32[]{:S(2)}, u32[]{:S(2)}) %collective-permute-start.10) | collective-permute-done | bytes 327712 | tf_op jit(solution)/shard_map/ppermute | solution.py:176
  116.9 2.2 %collective-permute-done.9 = bf16[4,2,2,32,640]{4,3,2,1,0:T(8,128)(2,1)} collective-permute-done((bf16[4,2,2,32,640]{4,3,2,1,0:T(8,128)(2,1)}, bf16[4,2,2,32,640]{4,3,2,1,0:T(8,128)(2,1)}, u32[]{:S(2)}, u32[]{:S(2)}) %collective-permute-start.9) | collective-permute-done | bytes 655392 | tf_op jit(solution)/shard_map/ppermute | solution.py:242
  119.1 5.5 %all-to-all-start.3 = ((bf16[8,2,32,640]{3,2,1,0:T(8,128)(2,1)}), bf16[8,2,32,640]{3,2,1,0:T(8,128)(2,1)}, u32[]{:S(2)}, u32[]{:S(2)}) async-start(bf16[8,2,32,640]{3,2,1,0:T(8,128)(2,1)} %bitcast.28), calls=%async_computation.3 | async-start | bytes 1310720 | tf_op jit(solution)/shard_map/all_to_all | solution.py:246
  124.6 0.2 select_reduce_fusion
  124.8 0.1 broadcast_select_fusion.1
  124.9 10.6 %project.1 = (f32[2,256,640]{2,1,0:T(8,128)S(1)}, f32[2,8,256]{2,1,0:T(8,128)S(1)}) custom-call(s32[16]{0:T(128)S(1)} %stack.67.order, bf16[2,320,256]{2,1,0:T(8,128)(2,1)} %get-tuple-element.44.refs_0_, bf16[2,320,256]{2,1,0:T(8,128)(2,1)} %collective-permute-done.refs_1_, bf16[2,320,256]{2,1,0:T(8,128)(2,1)} %collective-permute-done.1.refs_2_, ...), custom_call_target="tpu_custom_call" | custom-call | flops 3355443200 | bytes 13631488 | tf_op jit(solution)/shard_map/project/pallas_call | solution.py:90
  135.5 1.1 copy-done.1
  136.6 1.3 copy-done.2
  137.9 3.3 %attend.1 = f32[2,256]{1,0:T(2,128)S(1)} custom-call(s32[16]{0:T(128)S(1)} %broadcast_select_fusion.slot, f32[2,256,640]{2,1,0:T(8,128)S(1)} %copy-done.2, f32[2,8,256]{2,1,0:T(8,128)S(1)} %get-tuple-element.64.val, bf16[16,32,640]{2,1,0:T(8,128)(2,1)} %bitcast.27.near_ref, bf16[16,32,640]{2,1,0:T(8,128)(2,1)} %bitcast.29.far_ref), custom_call_target="tpu_custom_call" | custom-call | flops 503316480 | bytes 4194304 | tf_op jit(solution)/shard_map/attend/pallas_call | solution.py:142
  141.2 0.1 reshape.136
  141.3 0.2 select_reduce_fusion.2
  141.5 0.6 broadcast_in_dim.77
  142.1 3.4 %all-to-all-start.4 = ((f32[16,1,16]{2,1,0:T(1,128)}), f32[16,1,16]{2,1,0:T(1,128)S(1)}, u32[]{:S(2)}, u32[]{:S(2)}) async-start(f32[16,1,16]{2,1,0:T(1,128)} %broadcast_in_dim.77), calls=%async_computation.4 | async-start | bytes 16384 | tf_op jit(solution)/shard_map/all_to_all | solution.py:266
  145.5 0.1 convert_element_type.17
  145.6 7.8 %all-to-all-done.4 = f32[16,1,16]{2,1,0:T(1,128)S(1)} async-done(((f32[16,1,16]{2,1,0:T(1,128)}), f32[16,1,16]{2,1,0:T(1,128)S(1)}, u32[]{:S(2)}, u32[]{:S(2)}) %all-to-all-start.4) | async-done | bytes 1056 | tf_op jit(solution)/shard_map/all_to_all | solution.py:266
  153.4 0.1 reshape.138
  153.5 0.6 divide_select_fusion
  (38 shorter events, 0.2 us)
Async XLA Ops:
  6.5 1.9 %copy-start = (bf16[320,5120]{1,0:T(8,128)(2,1)S(1)}, bf16[320,5120]{1,0:T(8,128)(2,1)}, u32[]{:S(2)}) copy-start(bf16[320,5120]{1,0:T(8,128)(2,1)} %param.8) | copy-start | bytes 9830404
  7.5 23.3 %copy-start.4 = (s32[32]{0:T(128)}, s32[32]{0:T(128)S(1)}, u32[]{:S(2)}) copy-start(s32[32]{0:T(128)S(1)} %eq.81) | copy-start | bytes 388
  10.4 39.1 %all-to-all-start = ((bf16[16,48,640]{2,1,0:T(8,128)(2,1)}), bf16[16,48,640]{2,1,0:T(8,128)(2,1)}, u32[]{:S(2)}, u32[]{:S(2)}) async-start(bf16[16,48,640]{2,1,0:T(8,128)(2,1)} %maximum_maximum_fusion), calls=%async_computation | async-start | bytes 1966080 | tf_op jit(solution)/shard_map/all_to_all | solution.py:213
  18.9 106.0 %all-gather.3.cloned.1.call-start = ((), (), s32[]{:S(2)}) async-start(), calls=%async_computation.5 | async-start | bytes 7372800 | tf_op jit(solution)/shard_map/all_gather | solution.py:218
  20.9 36.3 %collective-permute-start.4 = (bf16[2,320,256]{2,1,0:T(8,128)(2,1)}, bf16[2,320,256]{2,1,0:T(8,128)(2,1)}, u32[]{:S(2)}, u32[]{:S(2)}) collective-permute-start(bf16[2,320,256]{2,1,0:T(8,128)(2,1)} %get-tuple-element.71), channel_id=1, source_target_pairs={{0,128},{64,192},{128,0},{192,64},{1,129},{65,193},{129,1},{193,65... | collective-permute-start | bytes 983048 | tf_op jit(solution)/shard_map/ppermute | solution.py:180
  23.7 33.6 %collective-permute-start.3 = (bf16[2,320,256]{2,1,0:T(8,128)(2,1)}, bf16[2,320,256]{2,1,0:T(8,128)(2,1)}, u32[]{:S(2)}, u32[]{:S(2)}) collective-permute-start(bf16[2,320,256]{2,1,0:T(8,128)(2,1)} %get-tuple-element.44.refs_0_), channel_id=1, source_target_pairs={{0,64},{64,0},{128,192},{192,128},{1,65},{65,1},{129,193},{193,129... | collective-permute-start | bytes 983048 | tf_op jit(solution)/shard_map/ppermute | solution.py:180
  25.2 32.1 %collective-permute-start.2 = (bf16[2,320,256]{2,1,0:T(8,128)(2,1)}, bf16[2,320,256]{2,1,0:T(8,128)(2,1)}, u32[]{:S(2)}, u32[]{:S(2)}) collective-permute-start(bf16[2,320,256]{2,1,0:T(8,128)(2,1)} %get-tuple-element.44.refs_0_), channel_id=1, source_target_pairs={{0,16},{16,32},{32,48},{48,0},{1,17},{17,33},{33,49},{49,1},{2,18}... | collective-permute-start | bytes 983048 | tf_op jit(solution)/shard_map/ppermute | solution.py:176
  26.6 30.6 %collective-permute-start.1 = (bf16[2,320,256]{2,1,0:T(8,128)(2,1)}, bf16[2,320,256]{2,1,0:T(8,128)(2,1)}, u32[]{:S(2)}, u32[]{:S(2)}) collective-permute-start(bf16[2,320,256]{2,1,0:T(8,128)(2,1)} %get-tuple-element.44.refs_0_), channel_id=1, source_target_pairs={{0,32},{16,48},{32,0},{48,16},{1,33},{17,49},{33,1},{49,17},{2,34}... | collective-permute-start | bytes 983048 | tf_op jit(solution)/shard_map/ppermute | solution.py:176
  29.3 28.0 %collective-permute-start = (bf16[2,320,256]{2,1,0:T(8,128)(2,1)}, bf16[2,320,256]{2,1,0:T(8,128)(2,1)}, u32[]{:S(2)}, u32[]{:S(2)}) collective-permute-start(bf16[2,320,256]{2,1,0:T(8,128)(2,1)} %get-tuple-element.44.refs_0_), channel_id=1, source_target_pairs={{0,48},{16,0},{32,16},{48,32},{1,49},{17,1},{33,17},{49,33},{2,50}... | collective-permute-start | bytes 983048 | tf_op jit(solution)/shard_map/ppermute | solution.py:176
  57.3 15.9 %collective-permute-start.7 = (bf16[2,320,256]{2,1,0:T(8,128)(2,1)}, bf16[2,320,256]{2,1,0:T(8,128)(2,1)}, u32[]{:S(2)}, u32[]{:S(2)}) collective-permute-start(bf16[2,320,256]{2,1,0:T(8,128)(2,1)} %collective-permute-done.3.refs_4_), channel_id=1, source_target_pairs={{0,16},{16,32},{32,48},{48,0},{1,17},{17,33},{33,49},{49,1},{2,18}... | collective-permute-start | bytes 983048 | tf_op jit(solution)/shard_map/ppermute | solution.py:176
  58.8 22.3 %collective-permute-start.6 = (bf16[2,320,256]{2,1,0:T(8,128)(2,1)}, bf16[2,320,256]{2,1,0:T(8,128)(2,1)}, u32[]{:S(2)}, u32[]{:S(2)}) collective-permute-start(bf16[2,320,256]{2,1,0:T(8,128)(2,1)} %collective-permute-done.3.refs_4_), channel_id=1, source_target_pairs={{0,32},{16,48},{32,0},{48,16},{1,33},{17,49},{33,1},{49,17},{2,34}... | collective-permute-start | bytes 983048 | tf_op jit(solution)/shard_map/ppermute | solution.py:176
  61.5 19.7 %collective-permute-start.5 = (bf16[2,320,256]{2,1,0:T(8,128)(2,1)}, bf16[2,320,256]{2,1,0:T(8,128)(2,1)}, u32[]{:S(2)}, u32[]{:S(2)}) collective-permute-start(bf16[2,320,256]{2,1,0:T(8,128)(2,1)} %collective-permute-done.3.refs_4_), channel_id=1, source_target_pairs={{0,48},{16,0},{32,16},{48,32},{1,49},{17,1},{33,17},{49,33},{2,50}... | collective-permute-start | bytes 983048 | tf_op jit(solution)/shard_map/ppermute | solution.py:176
  63.0 18.2 %collective-permute-start.8 = (bf16[2,320,256]{2,1,0:T(8,128)(2,1)}, bf16[2,320,256]{2,1,0:T(8,128)(2,1)}, u32[]{:S(2)}, u32[]{:S(2)}) collective-permute-start(bf16[2,320,256]{2,1,0:T(8,128)(2,1)} %collective-permute-done.4.refs_8_), channel_id=1, source_target_pairs={{0,64},{64,0},{128,192},{192,128},{1,65},{65,1},{129,193},{193,129... | collective-permute-start | bytes 983048 | tf_op jit(solution)/shard_map/ppermute | solution.py:180
  63.7 17.5 %all-to-all-start.1 = ((s32[16,1,48]{2,1,0:T(1,128)}), s32[16,1,48]{2,1,0:T(1,128)S(1)}, u32[]{:S(2)}, u32[]{:S(2)}) async-start(s32[16,1,48]{2,1,0:T(1,128)} %bitcast.5), calls=%async_computation.1 | async-start | bytes 16384 | tf_op jit(solution)/shard_map/all_to_all | solution.py:222
  72.6 22.2 %collective-permute-start.15 = (bf16[2,320,256]{2,1,0:T(8,128)(2,1)}, bf16[2,320,256]{2,1,0:T(8,128)(2,1)}, u32[]{:S(2)}, u32[]{:S(2)}) collective-permute-start(bf16[2,320,256]{2,1,0:T(8,128)(2,1)} %collective-permute-done.4.refs_8_), channel_id=1, source_target_pairs={{0,16},{16,32},{32,48},{48,0},{1,17},{17,33},{33,49},{49,1},{2,18}... | collective-permute-start | bytes 983048 | tf_op jit(solution)/shard_map/ppermute | solution.py:176
  73.2 22.2 %collective-permute-start.14 = (bf16[2,320,256]{2,1,0:T(8,128)(2,1)}, bf16[2,320,256]{2,1,0:T(8,128)(2,1)}, u32[]{:S(2)}, u32[]{:S(2)}) collective-permute-start(bf16[2,320,256]{2,1,0:T(8,128)(2,1)} %collective-permute-done.4.refs_8_), channel_id=1, source_target_pairs={{0,32},{16,48},{32,0},{48,16},{1,33},{17,49},{33,1},{49,17},{2,34}... | collective-permute-start | bytes 983048 | tf_op jit(solution)/shard_map/ppermute | solution.py:176
  81.8 2.6 %copy-start.3 = (bf16[16,32,5120]{2,1,0:T(8,128)(2,1)S(1)}, bf16[16,32,5120]{2,1,0:T(8,128)(2,1)}, u32[]{:S(2)}) copy-start(bf16[16,32,5120]{2,1,0:T(8,128)(2,1)} %q_ref.1) | copy-start | bytes 15728644
  85.9 6.6 %copy-start.6 = (s32[32]{0:T(128)S(1)}, s32[32]{0:T(128)}, u32[]{:S(2)}) copy-start(s32[32]{0:T(128)} %get-tuple-element.74) | copy-start | bytes 388
  87.1 37.5 %copy-start.5 = (s32[32]{0:T(128)S(1)}, s32[32]{0:T(128)}, u32[]{:S(2)}) copy-start(s32[32]{0:T(128)} %copy-done.4) | copy-start | bytes 388
  87.1 32.0 %collective-permute-start.9 = (bf16[4,2,2,32,640]{4,3,2,1,0:T(8,128)(2,1)}, bf16[4,2,2,32,640]{4,3,2,1,0:T(8,128)(2,1)}, u32[]{:S(2)}, u32[]{:S(2)}) collective-permute-start(bf16[4,2,2,32,640]{4,3,2,1,0:T(8,128)(2,1)} %get-tuple-element.70), channel_id=1, source_target_pairs={{0,194},{2,192},{64,130},{66,128},{128,66},{130,64},{192,2},{194,0... | collective-permute-start | bytes 1966088 | tf_op jit(solution)/shard_map/ppermute | solution.py:242
  87.1 29.8 %all-to-all-start.2 = ((bf16[8,2,32,640]{3,2,1,0:T(8,128)(2,1)}), bf16[8,2,32,640]{3,2,1,0:T(8,128)(2,1)}, u32[]{:S(2)}, u32[]{:S(2)}) async-start(bf16[8,2,32,640]{3,2,1,0:T(8,128)(2,1)} %bitcast.44), calls=%async_computation.2 | async-start | bytes 1310720 | tf_op jit(solution)/shard_map/all_to_all | solution.py:243
  92.6 10.9 %collective-permute-start.13 = (bf16[2,320,256]{2,1,0:T(8,128)(2,1)}, bf16[2,320,256]{2,1,0:T(8,128)(2,1)}, u32[]{:S(2)}, u32[]{:S(2)}) collective-permute-start(bf16[2,320,256]{2,1,0:T(8,128)(2,1)} %collective-permute-done.4.refs_8_), channel_id=1, source_target_pairs={{0,48},{16,0},{32,16},{48,32},{1,49},{17,1},{33,17},{49,33},{2,50}... | collective-permute-start | bytes 983048 | tf_op jit(solution)/shard_map/ppermute | solution.py:176
  92.8 18.3 %collective-permute-start.12 = (bf16[2,320,256]{2,1,0:T(8,128)(2,1)}, bf16[2,320,256]{2,1,0:T(8,128)(2,1)}, u32[]{:S(2)}, u32[]{:S(2)}) collective-permute-start(bf16[2,320,256]{2,1,0:T(8,128)(2,1)} %collective-permute-done.8.refs_12_), channel_id=1, source_target_pairs={{0,16},{16,32},{32,48},{48,0},{1,17},{17,33},{33,49},{49,1},{2,18}... | collective-permute-start | bytes 983048 | tf_op jit(solution)/shard_map/ppermute | solution.py:176
  94.7 16.4 %collective-permute-start.11 = (bf16[2,320,256]{2,1,0:T(8,128)(2,1)}, bf16[2,320,256]{2,1,0:T(8,128)(2,1)}, u32[]{:S(2)}, u32[]{:S(2)}) collective-permute-start(bf16[2,320,256]{2,1,0:T(8,128)(2,1)} %collective-permute-done.8.refs_12_), channel_id=1, source_target_pairs={{0,32},{16,48},{32,0},{48,16},{1,33},{17,49},{33,1},{49,17},{2,34}... | collective-permute-start | bytes 983048 | tf_op jit(solution)/shard_map/ppermute | solution.py:176
  95.4 21.5 %collective-permute-start.10 = (bf16[2,320,256]{2,1,0:T(8,128)(2,1)}, bf16[2,320,256]{2,1,0:T(8,128)(2,1)}, u32[]{:S(2)}, u32[]{:S(2)}) collective-permute-start(bf16[2,320,256]{2,1,0:T(8,128)(2,1)} %collective-permute-done.8.refs_12_), channel_id=1, source_target_pairs={{0,48},{16,0},{32,16},{48,32},{1,49},{17,1},{33,17},{49,33},{2,50}... | collective-permute-start | bytes 983048 | tf_op jit(solution)/shard_map/ppermute | solution.py:176
  119.1 17.5 %all-to-all-start.3 = ((bf16[8,2,32,640]{3,2,1,0:T(8,128)(2,1)}), bf16[8,2,32,640]{3,2,1,0:T(8,128)(2,1)}, u32[]{:S(2)}, u32[]{:S(2)}) async-start(bf16[8,2,32,640]{3,2,1,0:T(8,128)(2,1)} %bitcast.28), calls=%async_computation.3 | async-start | bytes 1310720 | tf_op jit(solution)/shard_map/all_to_all | solution.py:246
  135.5 1.1 copy-start.1
  136.6 16.9 %copy-start.7 = (s32[4]{0:T(128)S(1)}, s32[4]{0:T(128)}, u32[]{:S(2)}) copy-start(s32[4]{0:T(128)} %param.13) | copy-start | bytes 52
  136.6 1.3 copy-start.2
  142.1 11.3 %all-to-all-start.4 = ((f32[16,1,16]{2,1,0:T(1,128)}), f32[16,1,16]{2,1,0:T(1,128)S(1)}, u32[]{:S(2)}, u32[]{:S(2)}) async-start(f32[16,1,16]{2,1,0:T(1,128)} %broadcast_in_dim.77), calls=%async_computation.4 | async-start | bytes 16384 | tf_op jit(solution)/shard_map/all_to_all | solution.py:266
Sparse Core Ops, SparseCore 0:
  63.1 48.3 all-gather.2

commit v4 on v3

--- a/solution.py
+++ b/solution.py
@@ -49,7 +49,7 @@
         ],
         out_specs=pl.BlockSpec(memory_space=pltpu.VMEM),
         scratch_shapes=[pltpu.SemaphoreType.DMA((2 * CAP_DP,))],
-        compiler_params=pltpu.CompilerParams(vmem_limit_bytes=8 * 2**20),
+        compiler_params=pltpu.CompilerParams(vmem_limit_bytes=52 * 2**20),
         cost_estimate=pl.CostEstimate(flops=10**11, bytes_accessed=3 * 10**8, transcendentals=0),
         name="pick_queries",
     )(ids, col, queries)
@@ -109,9 +109,15 @@
     )(order, *units, w, v)
 
 
-def attend_kernel(slot, acc, val, near_ref, far_ref, o_ref, q_ref):
-    q_ref[0:CAP_DP] = near_ref[...]
-    q_ref[CAP_DP:] = far_ref[...]
+def attend_kernel(slot, acc, val, near_ref, far_ref, o_ref, q_ref, sem):
+    copies = [
+        pltpu.make_async_copy(near_ref, q_ref.at[pl.ds(0, CAP_DP)], sem.at[0]),
+        pltpu.make_async_copy(far_ref, q_ref.at[pl.ds(CAP_DP, CAP_DP)], sem.at[1]),
+    ]
+    for c in copies:
+        c.start()
+    for c in copies:
+        c.wait()
     scale = float(HD) ** (-0.5)
     part = functools.partial(
         lax.dot_general,
@@ -142,9 +148,13 @@
     return pl.pallas_call(
         attend_kernel,
         out_shape=jax.ShapeDtypeStruct((2, TOP * L), jnp.float32),
-        in_specs=[pl.BlockSpec(memory_space=pltpu.SMEM)] + [vmem] * 4,
+        in_specs=[pl.BlockSpec(memory_space=pltpu.SMEM), vmem, vmem]
+        + [pl.BlockSpec(memory_space=pltpu.HBM)] * 2,
         out_specs=vmem,
-        scratch_shapes=[pltpu.VMEM((2 * CAP_DP, L, GW), jnp.bfloat16)],
+        scratch_shapes=[
+            pltpu.VMEM((2 * CAP_DP, L, GW), jnp.bfloat16),
+            pltpu.SemaphoreType.DMA((2,)),
+        ],
         compiler_params=pltpu.CompilerParams(vmem_limit_bytes=40 * 2**20),
         cost_estimate=pl.CostEstimate(
             flops=2 * 3 * 10 * 256 * 256 * 128, bytes_accessed=4 * 2**20, transcendentals=655360

time: 162 us -> 160 us (0.988)
  local copies, waits for them, and re-layouts: 14.4 us -> 11.9 us
    unnamed x16 -> x14, local copies, waits for them, and re-layouts: 5.14 us -> 2.57 us
where the time goes in v4:
time: 160 us
  waiting for transfers between devices  58.2 us (36%)
  starting transfers between devices  54.7 us (34%)
  Pallas kernels  17.1 us (11%)
  between operations  13.7 us (9%)
  local copies, waits for them, and re-layouts  11.9 us (7%)
  other arithmetic  4.17 us (3%)
    ppermute x12, waiting for transfers between devices, shift(): return lax.ppermute(block, axis, [(i, (i + by) % 4) for i in range(4)])  18.5 us
    all_to_all x1, waiting for transfers between devices, local(): w_mine = lax.all_to_all(w_sent, TP, split_axis=0, concat_axis=0, tiled=True)  18.2 us
    ppermute x12, starting transfers between devices, shift(): return lax.ppermute(block, axis, [(i, (i + by) % 4) for i in range(4)])  18.1 us
    pallas_call x1, Pallas kernels, project(): pl.pallas_call(keys_kernel, out_shape=(jax.ShapeDtypeStruct((2, PATCH, GW...  10.6 us
    all_to_all x1, starting transfers between devices, local(): lax.all_to_all(notice, DP, split_axis=0, concat_axis=0, tiled=True)  8.86 us
    all_to_all x1, starting transfers between devices, local(): w_mine = lax.all_to_all(w_sent, TP, split_axis=0, concat_axis=0, tiled=True)  8.51 us
    all_to_all x1, waiting for transfers between devices, local(): lax.all_to_all(jnp.broadcast_to(sums[None], (16, 2 * TOP)), TP, split_axi...  7.78 us
    all_to_all x1, waiting for transfers between devices, local(): lax.all_to_all(notice, DP, split_axis=0, concat_axis=0, tiled=True)  6.88 us
  transfers between devices with their start and end apart: 22, of which 8 were waited for; matrix products, arithmetic and copies ran while one was open for 5% of the time, Pallas kernels for 8%

profile of v4, /device:TPU:8, one launch (start us, length us, event | category | flops | bytes accessed | tf_op | source)
XLA Modules:
  0.0 159.7 jit_solution(11481680383539783782)
XLA Ops:
  6.5 0.9 eq.81
  7.5 0.9 reshape.129
  8.3 0.2 copy-done
  8.6 0.7 pad_add_fusion
  9.3 1.0 maximum_maximum_fusion
  10.4 8.5 %all-to-all-start = ((bf16[16,48,640]{2,1,0:T(8,128)(2,1)}), bf16[16,48,640]{2,1,0:T(8,128)(2,1)}, u32[]{:S(2)}, u32[]{:S(2)}) async-start(bf16[16,48,640]{2,1,0:T(8,128)(2,1)} %maximum_maximum_fusion), calls=%async_computation | async-start | bytes 1966080 | tf_op jit(solution)/shard_map/all_to_all | solution.py:223
  18.9 0.0 all-gather.3.cloned.1.call-start
  19.0 2.0 %dynamic-slice_bitcast_fusion.1 = (bf16[2,320,256]{2,1,0:T(8,128)(2,1)}, bf16[2,320,256]{2,1,0:T(8,128)(2,1)}) fusion(bf16[256,4,320]{0,2,1:T(8,128)(2,1)} %param.7, s32[]{:T(128)S(6)} %select_n.153, s32[]{:T(128)S(6)} %select_n.152), kind=kLoop, calls=%fused_computation.3 | loop fusion | bytes 1310728 | tf_op jit(solution)/shard_map/dynamic_slice | solution.py:212
  20.9 2.8 %collective-permute-start.4 = (bf16[2,320,256]{2,1,0:T(8,128)(2,1)}, bf16[2,320,256]{2,1,0:T(8,128)(2,1)}, u32[]{:S(2)}, u32[]{:S(2)}) collective-permute-start(bf16[2,320,256]{2,1,0:T(8,128)(2,1)} %get-tuple-element.71), channel_id=1, source_target_pairs={{0,128},{64,192},{128,0},{192,64},{1,129},{65,193},{129,1},{193,65... | collective-permute-start | bytes 983048 | tf_op jit(solution)/shard_map/ppermute | solution.py:190
  23.7 1.5 collective-permute-start.3
  25.2 1.5 collective-permute-start.2
  26.6 2.7 %collective-permute-start.1 = (bf16[2,320,256]{2,1,0:T(8,128)(2,1)}, bf16[2,320,256]{2,1,0:T(8,128)(2,1)}, u32[]{:S(2)}, u32[]{:S(2)}) collective-permute-start(bf16[2,320,256]{2,1,0:T(8,128)(2,1)} %get-tuple-element.44.refs_0_), channel_id=1, source_target_pairs={{0,32},{16,48},{32,0},{48,16},{1,33},{17,49},{33,1},{49,17},{2,34}... | collective-permute-start | bytes 983048 | tf_op jit(solution)/shard_map/ppermute | solution.py:186
  29.3 1.5 collective-permute-start
  30.8 0.5 compare_select_fusion.4
  31.3 18.2 %all-to-all-done = bf16[16,48,640]{2,1,0:T(8,128)(2,1)} async-done(((bf16[16,48,640]{2,1,0:T(8,128)(2,1)}), bf16[16,48,640]{2,1,0:T(8,128)(2,1)}, u32[]{:S(2)}, u32[]{:S(2)}) %all-to-all-start) | async-done | bytes 983072 | tf_op jit(solution)/shard_map/all_to_all | solution.py:223
  49.4 0.9 slice.33.refs_17_
  50.4 2.1 %slice.32 = bf16[16,40,640]{2,1,0:T(8,128)(2,1)} slice(bf16[16,48,640]{2,1,0:T(8,128)(2,1)} %all-to-all-done), slice={[0:16], [0:40], [0:640]} | slice | bytes 1638400 | tf_op jit(solution)/shard_map/slice | solution.py:224
  52.5 4.8 %collective-permute-done.4.refs_8_ = bf16[2,320,256]{2,1,0:T(8,128)(2,1)} collective-permute-done((bf16[2,320,256]{2,1,0:T(8,128)(2,1)}, bf16[2,320,256]{2,1,0:T(8,128)(2,1)}, u32[]{:S(2)}, u32[]{:S(2)}) %collective-permute-start.4) | collective-permute-done | bytes 327712 | tf_op jit(solution)/shard_map/ppermute | solution.py:190
  57.3 1.5 collective-permute-start.7
  58.8 2.7 %collective-permute-start.6 = (bf16[2,320,256]{2,1,0:T(8,128)(2,1)}, bf16[2,320,256]{2,1,0:T(8,128)(2,1)}, u32[]{:S(2)}, u32[]{:S(2)}) collective-permute-start(bf16[2,320,256]{2,1,0:T(8,128)(2,1)} %collective-permute-done.3.refs_4_), channel_id=1, source_target_pairs={{0,32},{16,48},{32,0},{48,16},{1,33},{17,49},{33,1},{49,17},{2,34}... | collective-permute-start | bytes 983048 | tf_op jit(solution)/shard_map/ppermute | solution.py:186
  61.5 1.5 collective-permute-start.5
  63.0 0.0 all-gather.3.cloned.1.call-update
  63.0 0.1 collective-permute-start.8
  63.1 0.6 mark.3
  63.7 8.9 %all-to-all-start.1 = ((s32[16,1,48]{2,1,0:T(1,128)}), s32[16,1,48]{2,1,0:T(1,128)S(1)}, u32[]{:S(2)}, u32[]{:S(2)}) async-start(s32[16,1,48]{2,1,0:T(1,128)} %bitcast.5), calls=%async_computation.1 | async-start | bytes 16384 | tf_op jit(solution)/shard_map/all_to_all | solution.py:232
  72.6 0.6 collective-permute-start.15
  73.2 0.9 collective-permute-start.14
  74.1 6.9 %all-to-all-done.1 = s32[16,1,48]{2,1,0:T(1,128)S(1)} async-done(((s32[16,1,48]{2,1,0:T(1,128)}), s32[16,1,48]{2,1,0:T(1,128)S(1)}, u32[]{:S(2)}, u32[]{:S(2)}) %all-to-all-start.1) | async-done | bytes 3104 | tf_op jit(solution)/shard_map/all_to_all | solution.py:232
  81.0 0.3 convert_reduce_fusion
  81.4 0.1 select_reduce_fusion.1
  81.5 0.1 copy.16
  81.6 0.1 reshape.130.ids
  81.7 2.1 %pick_queries.1 = bf16[32,32,640]{2,1,0:T(8,128)(2,1)S(1)} custom-call(s32[32]{0:T(128)S(1)} %reshape.130.ids, s32[32]{0:T(128)S(1)} %get-tuple-element.73.col, bf16[16,32,5120]{2,1,0:T(8,128)(2,1)} %q_ref.1), custom_call_target="tpu_custom_call" | custom-call | flops 99999997952 | bytes 300000000 | tf_op jit(solution)/shard_map/pick_queries/pallas_call | solution.py:42
  83.8 0.0 copy-start.5
  83.9 1.2 constant_dynamic-slice_fusion
  85.1 5.8 %all-to-all-start.2 = ((bf16[8,2,32,640]{3,2,1,0:T(8,128)(2,1)}), bf16[8,2,32,640]{3,2,1,0:T(8,128)(2,1)}, u32[]{:S(2)}, u32[]{:S(2)}) async-start(bf16[8,2,32,640]{3,2,1,0:T(8,128)(2,1)} %bitcast.44), calls=%async_computation.2 | async-start | bytes 1310720 | tf_op jit(solution)/shard_map/all_to_all | solution.py:253
  90.9 0.2 convert_reduce_fusion.1
  91.0 0.1 collective-permute-start.13
  91.1 2.0 %collective-permute-start.12 = (bf16[2,320,256]{2,1,0:T(8,128)(2,1)}, bf16[2,320,256]{2,1,0:T(8,128)(2,1)}, u32[]{:S(2)}, u32[]{:S(2)}) collective-permute-start(bf16[2,320,256]{2,1,0:T(8,128)(2,1)} %collective-permute-done.8.refs_12_), channel_id=1, source_target_pairs={{0,16},{16,32},{32,48},{48,0},{1,17},{17,33},{33,49},{49,1},{2,18}... | collective-permute-start | bytes 983048 | tf_op jit(solution)/shard_map/ppermute | solution.py:186
  93.1 0.6 collective-permute-start.11
  93.8 2.6 %collective-permute-start.10 = (bf16[2,320,256]{2,1,0:T(8,128)(2,1)}, bf16[2,320,256]{2,1,0:T(8,128)(2,1)}, u32[]{:S(2)}, u32[]{:S(2)}) collective-permute-start(bf16[2,320,256]{2,1,0:T(8,128)(2,1)} %collective-permute-done.8.refs_12_), channel_id=1, source_target_pairs={{0,48},{16,0},{32,16},{48,32},{1,49},{17,1},{33,17},{49,33},{2,50}... | collective-permute-start | bytes 983048 | tf_op jit(solution)/shard_map/ppermute | solution.py:186
  96.5 0.1 stack.67.order
  96.6 0.1 broadcast_select_fusion.slot
  96.6 0.1 slice.26
  96.7 0.1 broadcast_in_dim.45
  96.8 5.2 %collective-permute-done.13.refs_9_ = bf16[2,320,256]{2,1,0:T(8,128)(2,1)} collective-permute-done((bf16[2,320,256]{2,1,0:T(8,128)(2,1)}, bf16[2,320,256]{2,1,0:T(8,128)(2,1)}, u32[]{:S(2)}, u32[]{:S(2)}) %collective-permute-start.13) | collective-permute-done | bytes 327712 | tf_op jit(solution)/shard_map/ppermute | solution.py:186
  102.0 7.5 %collective-permute-done.12.refs_15_ = bf16[2,320,256]{2,1,0:T(8,128)(2,1)} collective-permute-done((bf16[2,320,256]{2,1,0:T(8,128)(2,1)}, bf16[2,320,256]{2,1,0:T(8,128)(2,1)}, u32[]{:S(2)}, u32[]{:S(2)}) %collective-permute-start.12) | collective-permute-done | bytes 327712 | tf_op jit(solution)/shard_map/ppermute | solution.py:186
  109.5 5.8 %collective-permute-done.10.refs_13_ = bf16[2,320,256]{2,1,0:T(8,128)(2,1)} collective-permute-done((bf16[2,320,256]{2,1,0:T(8,128)(2,1)}, bf16[2,320,256]{2,1,0:T(8,128)(2,1)}, u32[]{:S(2)}, u32[]{:S(2)}) %collective-permute-start.10) | collective-permute-done | bytes 327712 | tf_op jit(solution)/shard_map/ppermute | solution.py:186
  115.3 2.0 %collective-permute-done.9 = bf16[4,2,2,32,640]{4,3,2,1,0:T(8,128)(2,1)} collective-permute-done((bf16[4,2,2,32,640]{4,3,2,1,0:T(8,128)(2,1)}, bf16[4,2,2,32,640]{4,3,2,1,0:T(8,128)(2,1)}, u32[]{:S(2)}, u32[]{:S(2)}) %collective-permute-start.9) | collective-permute-done | bytes 655392 | tf_op jit(solution)/shard_map/ppermute | solution.py:252
  117.3 5.5 %all-to-all-start.3 = ((bf16[8,2,32,640]{3,2,1,0:T(8,128)(2,1)}), bf16[8,2,32,640]{3,2,1,0:T(8,128)(2,1)}, u32[]{:S(2)}, u32[]{:S(2)}) async-start(bf16[8,2,32,640]{3,2,1,0:T(8,128)(2,1)} %bitcast.28), calls=%async_computation.3 | async-start | bytes 1310720 | tf_op jit(solution)/shard_map/all_to_all | solution.py:256
  122.8 0.2 select_reduce_fusion
  123.0 0.1 broadcast_select_fusion.1
  123.1 10.6 %project.1 = (f32[2,256,640]{2,1,0:T(8,128)S(1)}, f32[2,8,256]{2,1,0:T(8,128)S(1)}) custom-call(s32[16]{0:T(128)S(1)} %stack.67.order, bf16[2,320,256]{2,1,0:T(8,128)(2,1)} %get-tuple-element.44.refs_0_, bf16[2,320,256]{2,1,0:T(8,128)(2,1)} %collective-permute-done.refs_1_, bf16[2,320,256]{2,1,0:T(8,128)(2,1)} %collective-permute-done.1.refs_2_, ...), custom_call_target="tpu_custom_call" | custom-call | flops 3355443200 | bytes 13631488 | tf_op jit(solution)/shard_map/project/pallas_call | solution.py:90
  133.8 1.1 copy-done.1
  134.8 1.3 copy-done.2
  136.2 3.7 %attend.1 = f32[2,256]{1,0:T(2,128)S(1)} custom-call(s32[16]{0:T(128)S(1)} %broadcast_select_fusion.slot, f32[2,256,640]{2,1,0:T(8,128)S(1)} %copy-done.2, f32[2,8,256]{2,1,0:T(8,128)S(1)} %get-tuple-element.64.val, bf16[16,32,640]{2,1,0:T(8,128)(2,1)} %bitcast.27.near_ref, bf16[16,32,640]{2,1,0:T(8,128)(2,1)} %bitcast.29.far_ref), custom_call_target="tpu_custom_call" | custom-call | flops 503316480 | bytes 4194304 | tf_op jit(solution)/shard_map/attend/pallas_call | solution.py:148
  139.9 0.1 reshape.136
  140.0 0.2 select_reduce_fusion.2
  140.2 0.6 broadcast_in_dim.77
  140.8 3.5 %all-to-all-start.4 = ((f32[16,1,16]{2,1,0:T(1,128)}), f32[16,1,16]{2,1,0:T(1,128)S(1)}, u32[]{:S(2)}, u32[]{:S(2)}) async-start(f32[16,1,16]{2,1,0:T(1,128)} %broadcast_in_dim.77), calls=%async_computation.4 | async-start | bytes 16384 | tf_op jit(solution)/shard_map/all_to_all | solution.py:276
  144.3 0.1 convert_element_type.17
  144.3 7.8 %all-to-all-done.4 = f32[16,1,16]{2,1,0:T(1,128)S(1)} async-done(((f32[16,1,16]{2,1,0:T(1,128)}), f32[16,1,16]{2,1,0:T(1,128)S(1)}, u32[]{:S(2)}, u32[]{:S(2)}) %all-to-all-start.4) | async-done | bytes 1056 | tf_op jit(solution)/shard_map/all_to_all | solution.py:276
  152.1 0.1 reshape.138
  152.2 0.6 divide_select_fusion
  (36 shorter events, 0.2 us)
Async XLA Ops:
  6.5 1.9 %copy-start = (bf16[320,5120]{1,0:T(8,128)(2,1)S(1)}, bf16[320,5120]{1,0:T(8,128)(2,1)}, u32[]{:S(2)}) copy-start(bf16[320,5120]{1,0:T(8,128)(2,1)} %param.8) | copy-start | bytes 9830404
  7.5 23.3 %copy-start.3 = (s32[32]{0:T(128)}, s32[32]{0:T(128)S(1)}, u32[]{:S(2)}) copy-start(s32[32]{0:T(128)S(1)} %eq.81) | copy-start | bytes 388
  10.4 39.1 %all-to-all-start = ((bf16[16,48,640]{2,1,0:T(8,128)(2,1)}), bf16[16,48,640]{2,1,0:T(8,128)(2,1)}, u32[]{:S(2)}, u32[]{:S(2)}) async-start(bf16[16,48,640]{2,1,0:T(8,128)(2,1)} %maximum_maximum_fusion), calls=%async_computation | async-start | bytes 1966080 | tf_op jit(solution)/shard_map/all_to_all | solution.py:223
  18.9 104.2 %all-gather.3.cloned.1.call-start = ((), (), s32[]{:S(2)}) async-start(), calls=%async_computation.5 | async-start | bytes 7372800 | tf_op jit(solution)/shard_map/all_gather | solution.py:228
  20.9 36.3 %collective-permute-start.4 = (bf16[2,320,256]{2,1,0:T(8,128)(2,1)}, bf16[2,320,256]{2,1,0:T(8,128)(2,1)}, u32[]{:S(2)}, u32[]{:S(2)}) collective-permute-start(bf16[2,320,256]{2,1,0:T(8,128)(2,1)} %get-tuple-element.71), channel_id=1, source_target_pairs={{0,128},{64,192},{128,0},{192,64},{1,129},{65,193},{129,1},{193,65... | collective-permute-start | bytes 983048 | tf_op jit(solution)/shard_map/ppermute | solution.py:190
  23.7 33.6 %collective-permute-start.3 = (bf16[2,320,256]{2,1,0:T(8,128)(2,1)}, bf16[2,320,256]{2,1,0:T(8,128)(2,1)}, u32[]{:S(2)}, u32[]{:S(2)}) collective-permute-start(bf16[2,320,256]{2,1,0:T(8,128)(2,1)} %get-tuple-element.44.refs_0_), channel_id=1, source_target_pairs={{0,64},{64,0},{128,192},{192,128},{1,65},{65,1},{129,193},{193,129... | collective-permute-start | bytes 983048 | tf_op jit(solution)/shard_map/ppermute | solution.py:190
  25.2 32.1 %collective-permute-start.2 = (bf16[2,320,256]{2,1,0:T(8,128)(2,1)}, bf16[2,320,256]{2,1,0:T(8,128)(2,1)}, u32[]{:S(2)}, u32[]{:S(2)}) collective-permute-start(bf16[2,320,256]{2,1,0:T(8,128)(2,1)} %get-tuple-element.44.refs_0_), channel_id=1, source_target_pairs={{0,16},{16,32},{32,48},{48,0},{1,17},{17,33},{33,49},{49,1},{2,18}... | collective-permute-start | bytes 983048 | tf_op jit(solution)/shard_map/ppermute | solution.py:186
  26.6 30.6 %collective-permute-start.1 = (bf16[2,320,256]{2,1,0:T(8,128)(2,1)}, bf16[2,320,256]{2,1,0:T(8,128)(2,1)}, u32[]{:S(2)}, u32[]{:S(2)}) collective-permute-start(bf16[2,320,256]{2,1,0:T(8,128)(2,1)} %get-tuple-element.44.refs_0_), channel_id=1, source_target_pairs={{0,32},{16,48},{32,0},{48,16},{1,33},{17,49},{33,1},{49,17},{2,34}... | collective-permute-start | bytes 983048 | tf_op jit(solution)/shard_map/ppermute | solution.py:186
  29.3 28.0 %collective-permute-start = (bf16[2,320,256]{2,1,0:T(8,128)(2,1)}, bf16[2,320,256]{2,1,0:T(8,128)(2,1)}, u32[]{:S(2)}, u32[]{:S(2)}) collective-permute-start(bf16[2,320,256]{2,1,0:T(8,128)(2,1)} %get-tuple-element.44.refs_0_), channel_id=1, source_target_pairs={{0,48},{16,0},{32,16},{48,32},{1,49},{17,1},{33,17},{49,33},{2,50}... | collective-permute-start | bytes 983048 | tf_op jit(solution)/shard_map/ppermute | solution.py:186
  57.3 15.9 %collective-permute-start.7 = (bf16[2,320,256]{2,1,0:T(8,128)(2,1)}, bf16[2,320,256]{2,1,0:T(8,128)(2,1)}, u32[]{:S(2)}, u32[]{:S(2)}) collective-permute-start(bf16[2,320,256]{2,1,0:T(8,128)(2,1)} %collective-permute-done.3.refs_4_), channel_id=1, source_target_pairs={{0,16},{16,32},{32,48},{48,0},{1,17},{17,33},{33,49},{49,1},{2,18}... | collective-permute-start | bytes 983048 | tf_op jit(solution)/shard_map/ppermute | solution.py:186
  58.8 22.2 %collective-permute-start.6 = (bf16[2,320,256]{2,1,0:T(8,128)(2,1)}, bf16[2,320,256]{2,1,0:T(8,128)(2,1)}, u32[]{:S(2)}, u32[]{:S(2)}) collective-permute-start(bf16[2,320,256]{2,1,0:T(8,128)(2,1)} %collective-permute-done.3.refs_4_), channel_id=1, source_target_pairs={{0,32},{16,48},{32,0},{48,16},{1,33},{17,49},{33,1},{49,17},{2,34}... | collective-permute-start | bytes 983048 | tf_op jit(solution)/shard_map/ppermute | solution.py:186
  61.5 19.5 %collective-permute-start.5 = (bf16[2,320,256]{2,1,0:T(8,128)(2,1)}, bf16[2,320,256]{2,1,0:T(8,128)(2,1)}, u32[]{:S(2)}, u32[]{:S(2)}) collective-permute-start(bf16[2,320,256]{2,1,0:T(8,128)(2,1)} %collective-permute-done.3.refs_4_), channel_id=1, source_target_pairs={{0,48},{16,0},{32,16},{48,32},{1,49},{17,1},{33,17},{49,33},{2,50}... | collective-permute-start | bytes 983048 | tf_op jit(solution)/shard_map/ppermute | solution.py:186
  63.0 18.0 %collective-permute-start.8 = (bf16[2,320,256]{2,1,0:T(8,128)(2,1)}, bf16[2,320,256]{2,1,0:T(8,128)(2,1)}, u32[]{:S(2)}, u32[]{:S(2)}) collective-permute-start(bf16[2,320,256]{2,1,0:T(8,128)(2,1)} %collective-permute-done.4.refs_8_), channel_id=1, source_target_pairs={{0,64},{64,0},{128,192},{192,128},{1,65},{65,1},{129,193},{193,129... | collective-permute-start | bytes 983048 | tf_op jit(solution)/shard_map/ppermute | solution.py:190
  63.7 17.3 %all-to-all-start.1 = ((s32[16,1,48]{2,1,0:T(1,128)}), s32[16,1,48]{2,1,0:T(1,128)S(1)}, u32[]{:S(2)}, u32[]{:S(2)}) async-start(s32[16,1,48]{2,1,0:T(1,128)} %bitcast.5), calls=%async_computation.1 | async-start | bytes 16384 | tf_op jit(solution)/shard_map/all_to_all | solution.py:232
  72.6 20.6 %collective-permute-start.15 = (bf16[2,320,256]{2,1,0:T(8,128)(2,1)}, bf16[2,320,256]{2,1,0:T(8,128)(2,1)}, u32[]{:S(2)}, u32[]{:S(2)}) collective-permute-start(bf16[2,320,256]{2,1,0:T(8,128)(2,1)} %collective-permute-done.4.refs_8_), channel_id=1, source_target_pairs={{0,16},{16,32},{32,48},{48,0},{1,17},{17,33},{33,49},{49,1},{2,18}... | collective-permute-start | bytes 983048 | tf_op jit(solution)/shard_map/ppermute | solution.py:186
  73.2 20.5 %collective-permute-start.14 = (bf16[2,320,256]{2,1,0:T(8,128)(2,1)}, bf16[2,320,256]{2,1,0:T(8,128)(2,1)}, u32[]{:S(2)}, u32[]{:S(2)}) collective-permute-start(bf16[2,320,256]{2,1,0:T(8,128)(2,1)} %collective-permute-done.4.refs_8_), channel_id=1, source_target_pairs={{0,32},{16,48},{32,0},{48,16},{1,33},{17,49},{33,1},{49,17},{2,34}... | collective-permute-start | bytes 983048 | tf_op jit(solution)/shard_map/ppermute | solution.py:186
  83.8 7.0 %copy-start.5 = (s32[32]{0:T(128)S(1)}, s32[32]{0:T(128)}, u32[]{:S(2)}) copy-start(s32[32]{0:T(128)} %get-tuple-element.74) | copy-start | bytes 388
  85.1 37.8 %copy-start.4 = (s32[32]{0:T(128)S(1)}, s32[32]{0:T(128)}, u32[]{:S(2)}) copy-start(s32[32]{0:T(128)} %copy-done.3) | copy-start | bytes 388
  85.1 32.2 %collective-permute-start.9 = (bf16[4,2,2,32,640]{4,3,2,1,0:T(8,128)(2,1)}, bf16[4,2,2,32,640]{4,3,2,1,0:T(8,128)(2,1)}, u32[]{:S(2)}, u32[]{:S(2)}) collective-permute-start(bf16[4,2,2,32,640]{4,3,2,1,0:T(8,128)(2,1)} %get-tuple-element.70), channel_id=1, source_target_pairs={{0,194},{2,192},{64,130},{66,128},{128,66},{130,64},{192,2},{194,0... | collective-permute-start | bytes 1966088 | tf_op jit(solution)/shard_map/ppermute | solution.py:252
  85.1 30.2 %all-to-all-start.2 = ((bf16[8,2,32,640]{3,2,1,0:T(8,128)(2,1)}), bf16[8,2,32,640]{3,2,1,0:T(8,128)(2,1)}, u32[]{:S(2)}, u32[]{:S(2)}) async-start(bf16[8,2,32,640]{3,2,1,0:T(8,128)(2,1)} %bitcast.44), calls=%async_computation.2 | async-start | bytes 1310720 | tf_op jit(solution)/shard_map/all_to_all | solution.py:253
  91.0 10.9 %collective-permute-start.13 = (bf16[2,320,256]{2,1,0:T(8,128)(2,1)}, bf16[2,320,256]{2,1,0:T(8,128)(2,1)}, u32[]{:S(2)}, u32[]{:S(2)}) collective-permute-start(bf16[2,320,256]{2,1,0:T(8,128)(2,1)} %collective-permute-done.4.refs_8_), channel_id=1, source_target_pairs={{0,48},{16,0},{32,16},{48,32},{1,49},{17,1},{33,17},{49,33},{2,50}... | collective-permute-start | bytes 983048 | tf_op jit(solution)/shard_map/ppermute | solution.py:186
  91.1 18.4 %collective-permute-start.12 = (bf16[2,320,256]{2,1,0:T(8,128)(2,1)}, bf16[2,320,256]{2,1,0:T(8,128)(2,1)}, u32[]{:S(2)}, u32[]{:S(2)}) collective-permute-start(bf16[2,320,256]{2,1,0:T(8,128)(2,1)} %collective-permute-done.8.refs_12_), channel_id=1, source_target_pairs={{0,16},{16,32},{32,48},{48,0},{1,17},{17,33},{33,49},{49,1},{2,18}... | collective-permute-start | bytes 983048 | tf_op jit(solution)/shard_map/ppermute | solution.py:186
  93.1 16.4 %collective-permute-start.11 = (bf16[2,320,256]{2,1,0:T(8,128)(2,1)}, bf16[2,320,256]{2,1,0:T(8,128)(2,1)}, u32[]{:S(2)}, u32[]{:S(2)}) collective-permute-start(bf16[2,320,256]{2,1,0:T(8,128)(2,1)} %collective-permute-done.8.refs_12_), channel_id=1, source_target_pairs={{0,32},{16,48},{32,0},{48,16},{1,33},{17,49},{33,1},{49,17},{2,34}... | collective-permute-start | bytes 983048 | tf_op jit(solution)/shard_map/ppermute | solution.py:186
  93.8 21.5 %collective-permute-start.10 = (bf16[2,320,256]{2,1,0:T(8,128)(2,1)}, bf16[2,320,256]{2,1,0:T(8,128)(2,1)}, u32[]{:S(2)}, u32[]{:S(2)}) collective-permute-start(bf16[2,320,256]{2,1,0:T(8,128)(2,1)} %collective-permute-done.8.refs_12_), channel_id=1, source_target_pairs={{0,48},{16,0},{32,16},{48,32},{1,49},{17,1},{33,17},{49,33},{2,50}... | collective-permute-start | bytes 983048 | tf_op jit(solution)/shard_map/ppermute | solution.py:186
  117.3 17.5 %all-to-all-start.3 = ((bf16[8,2,32,640]{3,2,1,0:T(8,128)(2,1)}), bf16[8,2,32,640]{3,2,1,0:T(8,128)(2,1)}, u32[]{:S(2)}, u32[]{:S(2)}) async-start(bf16[8,2,32,640]{3,2,1,0:T(8,128)(2,1)} %bitcast.28), calls=%async_computation.3 | async-start | bytes 1310720 | tf_op jit(solution)/shard_map/all_to_all | solution.py:256
  133.8 1.1 copy-start.1
  134.8 17.4 %copy-start.6 = (s32[4]{0:T(128)S(1)}, s32[4]{0:T(128)}, u32[]{:S(2)}) copy-start(s32[4]{0:T(128)} %param.13) | copy-start | bytes 52
  134.8 1.3 copy-start.2
  140.8 11.4 %all-to-all-start.4 = ((f32[16,1,16]{2,1,0:T(1,128)}), f32[16,1,16]{2,1,0:T(1,128)S(1)}, u32[]{:S(2)}, u32[]{:S(2)}) async-start(f32[16,1,16]{2,1,0:T(1,128)} %broadcast_in_dim.77), calls=%async_computation.4 | async-start | bytes 16384 | tf_op jit(solution)/shard_map/all_to_all | solution.py:276
Sparse Core Ops, SparseCore 0:
  63.1 48.4 all-gather.2
